TPU v7x, 128 devices: a whole 4x4x4 slice. The times are simulated.
128 devices in a mesh: dp: 4 (over z_hi, core), seq: 32 (over z_lo, x, y).
Axes of the slice: x: 4, y: 4, z: 4 (z_hi: 2, z_lo: 2; z = z_hi * 2 + z_lo), core: 2. Of those that a mesh axis runs over, the one named last changes fastest.
Arguments:
- head_inputs: bfloat16 [4, 8192, 8192], P('dp', 'seq'), may hold values from -6 to 6
- write_proj: bfloat16 [4, 8192, 1024], P('dp', 'seq'), may hold values from -6 to 6
- read_projection: bfloat16 [4, 8192, 1024], P('dp', 'seq'), may hold values from -0.5 to 0.5
- step_raw: bfloat16 [4, 8192, 128], P('dp', 'seq'), may hold values from -2 to 12
- output_grad: bfloat16 [4, 8192, 8192], P('dp', 'seq'), may hold values from -1.5 to 1.5
- decay_log: float32 [128], P('seq'), may hold values from -0.7 to 1.4
- step_bias: float32 [128], P('seq'), may hold values from -14 to -2
- skip_gain: float32 [128], P('seq'), may hold values from 0.5 to 1.5
Outputs:
- input_grad: bfloat16 [4, 8192, 8192], P('dp', 'seq')
- write_grad: bfloat16 [4, 8192, 1024], P('dp', 'seq')
- read_grad: bfloat16 [4, 8192, 1024], P('dp', 'seq')
- step_grad: bfloat16 [4, 8192, 128], P('dp', 'seq')
- head_gradients: float32 [3, 128], P(None, 'seq')
All inputs are finite; a program needn't handle non-finite values.
Results may differ from a plain program's by a relative error of at most 0.023.
Values may be sent and summed in bfloat16 or wider, within the bound.
A program may use at most 640 MiB of HBM per device.

v0:
```python
import math

import jax
import jax.numpy as jnp
from jax import lax
from jax.sharding import PartitionSpec as P

HEADDIM = 64
NSTATE = 128
BLOCK = 256


HIGH = lax.Precision.HIGHEST
BF = jnp.bfloat16
FL = jnp.float32


def spanned_scan(
    inputs, writes, readout, step_raw, step_bias, decay_log, skip_gain, start_state, block_len
):
    seq_len = inputs.shape[0]
    blocks = seq_len // block_len
    step_size = jax.nn.softplus(step_raw + step_bias)
    decays = step_size * -jnp.exp(decay_log)
    input_blk = inputs.reshape(blocks, block_len, -1)
    write_blk = writes.reshape(blocks, block_len, -1)
    read_blk = readout.reshape(blocks, block_len, -1)
    step_blk = step_size.reshape(blocks, block_len)
    within = jnp.cumsum(decays.reshape(blocks, block_len), axis=1)
    lower_mask = jnp.tril(jnp.ones((block_len, block_len), dtype=bool))
    log_gaps = jnp.where(lower_mask, within[:, :, None] - within[:, None, :], -1e30)
    raw_scores = jnp.einsum("cin,cjn->cij", read_blk, write_blk, preferred_element_type=FL)
    weights = (raw_scores * jnp.exp(log_gaps) * step_blk[:, None, :]).astype(BF)
    local_out = jnp.einsum("cij,cjp->cip", weights, input_blk, preferred_element_type=FL)
    to_end = jnp.exp(within[:, -1:] - within) * step_blk
    scaled_writes = (write_blk.astype(FL) * to_end[:, :, None]).astype(BF)
    block_states = jnp.einsum("cjn,cjp->cpn", scaled_writes, input_blk, preferred_element_type=FL)
    block_boundaries = jnp.cumsum(jnp.concatenate([jnp.zeros((1,), within.dtype), within[:, -1]]))
    lower_blocks = jnp.tril(jnp.ones((blocks + 1, blocks + 1), dtype=bool))
    carry_decay = jnp.exp(
        jnp.where(lower_blocks, block_boundaries[:, None] - block_boundaries[None, :], -1e30)
    )
    stacked = jnp.concatenate([start_state[None], block_states], axis=0)
    carried = jnp.einsum("cd,dpn->cpn", carry_decay, stacked, precision=HIGH)
    carried_b = carried[:-1].astype(BF)
    carried_output = (
        jnp.einsum("cin,cpn->cip", read_blk, carried_b, preferred_element_type=FL)
        * jnp.exp(within)[:, :, None]
    )
    outputs = (local_out + carried_output).reshape(seq_len, -1) + skip_gain * inputs.astype(FL)
    return (outputs, carried[-1])


def head_backward(
    inputs,
    writes,
    readout,
    step_raw,
    output_grad,
    step_bias,
    decay_log,
    skip_gain,
    start_state,
    end_grad,
    block_len,
):

    def forward(
        in_rows, write_rows, read_rows, raw_rows, bias_value, decay_value, skip_value, state_value
    ):
        return spanned_scan(
            in_rows,
            write_rows,
            read_rows,
            raw_rows,
            bias_value,
            decay_value,
            skip_value,
            state_value,
            block_len,
        )

    _, pullback = jax.vjp(
        forward, inputs, writes, readout, step_raw, step_bias, decay_log, skip_gain, start_state
    )
    return pullback((output_grad, end_grad))


def over_heads(function, arrays, block_size):
    head_total = arrays[0].shape[0]
    shaped = tuple(
        (
            member.reshape((head_total // block_size, block_size) + member.shape[1:])
            for member in arrays
        )
    )
    result = lax.map(lambda group_args: jax.vmap(function)(*group_args), shaped)
    return jax.tree.map(
        lambda stacked_out: stacked_out.reshape((head_total,) + stacked_out.shape[2:]), result
    )


def body(
    head_inputs, write_proj, read_projection, step_raw, output_grad, decay_log, step_bias, skip_gain
):
    dev_count = lax.axis_size("seq")
    tok_rows = head_inputs.shape[1]
    head_total = step_raw.shape[2]
    group_total = write_proj.shape[2] // NSTATE
    seq_len = tok_rows * dev_count
    factor = 1.0 / math.sqrt(lax.axis_size("dp") * seq_len * HEADDIM)
    owned = head_total // dev_count
    own_width = owned * HEADDIM
    input_rows = head_inputs.reshape(tok_rows, dev_count, own_width)
    grad_rows = output_grad.reshape(tok_rows, dev_count, own_width)
    proj_rows = jnp.concatenate(
        [
            write_proj.reshape(tok_rows, group_total, NSTATE),
            read_projection.reshape(tok_rows, group_total, NSTATE),
        ],
        axis=2,
    )
    proj_rows = jnp.repeat(proj_rows, dev_count // group_total, axis=1)
    rate_rows = step_raw.reshape(tok_rows, dev_count, owned)
    input_own, proj_own, rate_own, grad_own = (
        lax.all_to_all(input_rows, "seq", split_axis=1, concat_axis=0, tiled=True),
        lax.all_to_all(proj_rows, "seq", split_axis=1, concat_axis=0, tiled=True),
        lax.all_to_all(rate_rows, "seq", split_axis=1, concat_axis=0, tiled=True),
        lax.all_to_all(grad_rows, "seq", split_axis=1, concat_axis=0, tiled=True),
    )
    write_own = proj_own[:, 0, :NSTATE]
    read_own = proj_own[:, 0, NSTATE:]
    zero_state = jnp.zeros((HEADDIM, NSTATE), jnp.float32)

    def one_head(inputs, rate_seq, grad_seq, decay_value, step_shift, skip_scale):
        pulled = head_backward(
            inputs,
            write_own,
            read_own,
            rate_seq.astype(FL),
            grad_seq.astype(FL),
            step_shift,
            decay_value,
            skip_scale,
            zero_state,
            zero_state,
            BLOCK,
        )
        return (
            pulled[0],
            pulled[1].astype(FL),
            pulled[2].astype(FL),
            pulled[3].astype(BF),
            jnp.stack([pulled[5], pulled[4], pulled[6]]),
        )

    head_arrays = (
        input_own.reshape(seq_len, owned, HEADDIM).transpose(1, 0, 2),
        rate_own.reshape(seq_len, owned).T,
        grad_own.reshape(seq_len, owned, HEADDIM).transpose(1, 0, 2),
        decay_log,
        step_bias,
        skip_gain,
    )
    grad_input, grad_write, grad_read, grad_rate, grad_params = over_heads(
        one_head, head_arrays, math.gcd(owned, max(1, 8192 // seq_len))
    )
    input_back = grad_input.transpose(1, 0, 2).reshape(seq_len, 1, own_width)
    rate_back = grad_rate.T.reshape(seq_len, 1, owned)
    input_home, rate_home = (
        lax.all_to_all(input_back, "seq", split_axis=0, concat_axis=1, tiled=True),
        lax.all_to_all(rate_back, "seq", split_axis=0, concat_axis=1, tiled=True),
    )
    proj_sums = jnp.concatenate(
        [jnp.sum(grad_write, axis=0), jnp.sum(grad_read, axis=0)], axis=1
    ).reshape(seq_len, 1, 2 * NSTATE)
    proj_home = lax.all_to_all(proj_sums, "seq", split_axis=0, concat_axis=1, tiled=True)
    proj_home = jnp.sum(
        proj_home.reshape(tok_rows, group_total, dev_count // group_total, 2 * NSTATE), axis=2
    )
    input_grad = input_home.reshape(1, tok_rows, head_total * HEADDIM)
    step_grad = rate_home.reshape(1, tok_rows, head_total)
    write_grad = proj_home[:, :, :NSTATE].reshape(1, tok_rows, group_total * NSTATE).astype(BF)
    read_grad = proj_home[:, :, NSTATE:].reshape(1, tok_rows, group_total * NSTATE).astype(BF)
    head_gradients = lax.psum(grad_params.T, "dp") * factor
    return (input_grad, write_grad, read_grad, step_grad, head_gradients)


def solution(mesh):
    return jax.shard_map(
        body,
        mesh=mesh,
        in_specs=(
            P("dp", "seq", None),
            P("dp", "seq", None),
            P("dp", "seq", None),
            P("dp", "seq", None),
            P("dp", "seq", None),
            P("seq"),
            P("seq"),
            P("seq"),
        ),
        out_specs=(
            P("dp", "seq", None),
            P("dp", "seq", None),
            P("dp", "seq", None),
            P("dp", "seq", None),
            P(None, "seq"),
        ),
        check_vma=False,
    )
```

profile of v0, /device:TPU:54, one launch (start us, length us, event | category | flops | bytes accessed | tf_op | source)
XLA Modules:
  0.0 928.8 jit_solution(4379593338945997485)
XLA Ops:
  5.8 8.4 all-to-all-start.2
  14.2 6.4 copy.349
  20.6 48.9 %all-to-all-done.2 = bf16[256,32,256]{2,0,1:T(8,128)(2,1)} async-done(((bf16[256,32,256]{2,0,1:T(8,128)(2,1)}), bf16[256,32,256]{2,0,1:T(8,128)(2,1)}, u32[]{:S(2)}, u32[]{:S(2)}) %all-to-all-start.2) | async-done | bytes 4194336 | tf_op jit(solution)/shard_map/all_to_all | solution.py:127
  69.5 9.1 all-to-all-start.3
  78.6 6.4 copy.345
  85.0 48.9 %all-to-all-done.3 = bf16[256,32,256]{0,2,1:T(8,128)(2,1)} async-done(((bf16[256,32,256]{0,2,1:T(8,128)(2,1)}), bf16[256,32,256]{0,2,1:T(8,128)(2,1)}, u32[]{:S(2)}, u32[]{:S(2)}) %all-to-all-start.3) | async-done | bytes 4194336 | tf_op jit(solution)/shard_map/all_to_all | solution.py:126
  134.0 9.3 all-to-all-start
  144.1 54.5 %all-to-all-done = bf16[256,32,256]{0,2,1:T(8,128)(2,1)} async-done(((bf16[256,32,256]{0,2,1:T(8,128)(2,1)}), bf16[256,32,256]{0,2,1:T(8,128)(2,1)}, u32[]{:S(2)}, u32[]{:S(2)}) %all-to-all-start) | async-done | bytes 4194336 | tf_op jit(solution)/shard_map/all_to_all | solution.py:129
  198.6 9.1 all-to-all-start.1
  211.4 6.5 copy.350
  217.9 7.4 reshape.1283
  225.3 6.5 copy.346
  231.8 7.4 reshape.1272
  239.3 443.7 %while.18 = (s32[]{:T(128)}, bf16[4,1,8192,64]{2,3,1,0:T(8,128)(2,1)}, f32[4,1,8192,128]{3,2,1,0:T(8,128)}, f32[4,1,8192,128]{3,2,1,0:T(8,128)}, bf16[4,1,8192]{...) while((s32[]{:T(128)}, ...), condition=%wide.region_18.19_spmd, body=%wide.region_0.18_spmd.sunk | while | flops 3365396480 | bytes 204569824 | solution.py:97
  279.7 5.1 fusion.196
  305.7 8.6 fusion.204
  314.4 5.6 copy.513
  327.0 5.1 fusion.197
  357.0 6.0 convert_dynamic-update-slice_fusion.2
  383.8 5.1 fusion.196
  409.8 8.6 fusion.204
  418.4 5.6 copy.513
  461.0 6.1 convert_dynamic-update-slice_fusion.2
  488.0 5.1 fusion.196
  513.9 8.6 fusion.204
  522.6 5.6 copy.513
  565.2 6.2 convert_dynamic-update-slice_fusion.2
  592.2 5.1 fusion.196
  618.1 8.6 fusion.204
  626.8 5.6 copy.513
  669.4 6.0 convert_dynamic-update-slice_fusion.2
  690.8 8.3 all-to-all-start.6
  699.1 6.8 reduce.40
  705.9 6.4 copy.448
  712.2 6.9 reshape.1318
  719.2 8.4 all-to-all-start.4
  727.5 9.1 reduce_sum.158
  736.6 9.2 reduce_sum.159
  749.8 6.9 reshape.1288
  756.7 21.5 %all-to-all-done.4 = bf16[32,2,32768]{2,1,0:T(2,128)(2,1)} async-done(((bf16[32,2,32768]{2,1,0:T(2,128)(2,1)}), bf16[32,2,32768]{2,1,0:T(2,128)(2,1)}, u32[]{:S(2)}, u32[]{:S(2)}) %all-to-all-start.4) | async-done | bytes 4194336 | tf_op jit(solution)/shard_map/all_to_all | solution.py:171
  778.2 9.4 %all-to-all-start.5 = ((f32[8192,1,256]{2,1,0:T(1,128)}), f32[8192,1,256]{2,1,0:T(1,128)}, u32[]{:S(2)}, u32[]{:S(2)}) async-start(f32[8192,1,256]{2,1,0:T(1,128)} %reshape.1288), calls=%async_computation.5 | async-start | bytes 16777216 | tf_op jit(solution)/shard_map/all_to_all | solution.py:177
  787.6 76.5 %psum.7 = f32[3,4]{0,1:T(4,128)S(1)} all-reduce(f32[3,4]{0,1:T(4,128)S(1)} %bitcast.491), channel_id=1, replica_groups=mesh['dp'=4,'seq'=32] {'dp'}, use_global_device_ids=true, to_apply=%region_22.23 | all-reduce | flops 12 | bytes 96 | tf_op jit(solution)/shard_map/psum | solution.py:185
  864.8 8.7 reshape.1321
  873.4 8.1 copy.359
  882.4 19.8 %reshape.1319 = bf16[8192,1,256]{2,1,0:T(2,128)(2,1)} reshape(bf16[32,2,32768]{2,1,0:T(2,128)(2,1)} %all-to-all-done.4) | data formatting | bytes 8388608
  902.2 6.1 copy.371
  908.3 6.4 copy.355
  914.7 6.3 copy.361
  (535 shorter events, 330.8 us)
Async XLA Ops:
  5.8 63.7 %all-to-all-start.2 = ((bf16[256,32,256]{2,0,1:T(8,128)(2,1)}), bf16[256,32,256]{2,0,1:T(8,128)(2,1)}, u32[]{:S(2)}, u32[]{:S(2)}) async-start(bf16[256,32,256]{2,0,1:T(8,128)(2,1)} %bitcast.461), calls=%async_computation.2 | async-start | bytes 8388608 | tf_op jit(solution)/shard_map/all_to_all | solution.py:127
  69.5 64.5 %all-to-all-start.3 = ((bf16[256,32,256]{0,2,1:T(8,128)(2,1)}), bf16[256,32,256]{0,2,1:T(8,128)(2,1)}, u32[]{:S(2)}, u32[]{:S(2)}) async-start(bf16[256,32,256]{0,2,1:T(8,128)(2,1)} %bitcast.463), calls=%async_computation.3 | async-start | bytes 8388608 | tf_op jit(solution)/shard_map/all_to_all | solution.py:126
  134.0 9.3 %copy-start.23 = (bf16[1,256,128]{2,1,0:T(8,128)(2,1)S(1)}, bf16[1,256,128]{2,1,0:T(8,128)(2,1)}, u32[]{:S(2)}) copy-start(bf16[1,256,128]{2,1,0:T(8,128)(2,1)} %param.13) | copy-start | bytes 196612
  134.0 64.6 %all-to-all-start = ((bf16[256,32,256]{0,2,1:T(8,128)(2,1)}), bf16[256,32,256]{0,2,1:T(8,128)(2,1)}, u32[]{:S(2)}, u32[]{:S(2)}) async-start(bf16[256,32,256]{0,2,1:T(8,128)(2,1)} %bitcast.462), calls=%async_computation | async-start | bytes 8388608 | tf_op jit(solution)/shard_map/all_to_all | solution.py:129
  198.6 40.7 %all-to-all-start.1 = ((bf16[256,32,4]{0,2,1:T(4,128)(2,1)}), bf16[256,32,4]{0,2,1:T(4,128)(2,1)S(1)}, u32[]{:S(2)}, u32[]{:S(2)}) async-start(bf16[256,32,4]{0,2,1:T(4,128)(2,1)} %reshape.1274), calls=%async_computation.1 | async-start | bytes 131072 | tf_op jit(solution)/shard_map/all_to_all | solution.py:128
  231.8 7.5 copy-start.25
  231.8 7.5 copy-start.27
  231.8 7.5 copy-start.29
  264.6 20.3 %copy-start.20 = (f32[32]{0:T(128)}, f32[32]{0:T(128)S(1)}, u32[]{:S(2)}) copy-start(f32[32]{0:T(128)S(1)} %slice_reduce_fusion.7) | copy-start | bytes 388 | tf_op jit(solution)/shard_map/while
  285.6 34.3 %copy-start.14 = (f32[32,256]{1,0:T(8,128)}, f32[32,256]{1,0:T(8,128)S(1)}, u32[]{:S(2)}) copy-start(f32[32,256]{1,0:T(8,128)S(1)} %get-tuple-element.369) | copy-start | bytes 98308 | tf_op jit(solution)/shard_map/while
  319.9 7.1 copy-start.8
  336.7 12.6 %copy-start.22 = (f32[32]{0:T(128)S(1)}, f32[32]{0:T(128)}, u32[]{:S(2)}) copy-start(f32[32]{0:T(128)} %copy-done.20) | copy-start | bytes 388 | tf_op jit(solution)/shard_map/while
  336.7 17.0 %copy-start.2 = (bf16[1,1,8192,64]{2,3,1,0:T(8,128)(2,1)S(1)}, bf16[1,1,8192,64]{2,3,1,0:T(8,128)(2,1)}, u32[]{:S(2)}) copy-start(bf16[1,1,8192,64]{2,3,1,0:T(8,128)(2,1)} %copy-done.1) | copy-start | bytes 3145732 | tf_op jit(solution)/shard_map/while
  356.9 6.0 copy-start.18
  356.9 6.0 copy-start.26
  356.9 6.0 copy-start.28
  357.0 6.0 copy-start.30
  368.7 20.3 %copy-start.20 = (f32[32]{0:T(128)}, f32[32]{0:T(128)S(1)}, u32[]{:S(2)}) copy-start(f32[32]{0:T(128)S(1)} %slice_reduce_fusion.7) | copy-start | bytes 388 | tf_op jit(solution)/shard_map/while
  389.7 34.3 %copy-start.14 = (f32[32,256]{1,0:T(8,128)}, f32[32,256]{1,0:T(8,128)S(1)}, u32[]{:S(2)}) copy-start(f32[32,256]{1,0:T(8,128)S(1)} %get-tuple-element.369) | copy-start | bytes 98308 | tf_op jit(solution)/shard_map/while
  424.0 7.1 copy-start.8
  440.7 12.6 %copy-start.22 = (f32[32]{0:T(128)S(1)}, f32[32]{0:T(128)}, u32[]{:S(2)}) copy-start(f32[32]{0:T(128)} %copy-done.20) | copy-start | bytes 388 | tf_op jit(solution)/shard_map/while
  440.8 17.0 %copy-start.2 = (bf16[1,1,8192,64]{2,3,1,0:T(8,128)(2,1)S(1)}, bf16[1,1,8192,64]{2,3,1,0:T(8,128)(2,1)}, u32[]{:S(2)}) copy-start(bf16[1,1,8192,64]{2,3,1,0:T(8,128)(2,1)} %copy-done.1) | copy-start | bytes 3145732 | tf_op jit(solution)/shard_map/while
  461.0 6.1 copy-start.18
  461.0 6.1 copy-start.26
  461.0 6.1 copy-start.28
  461.0 6.1 copy-start.30
  472.8 20.3 %copy-start.20 = (f32[32]{0:T(128)}, f32[32]{0:T(128)S(1)}, u32[]{:S(2)}) copy-start(f32[32]{0:T(128)S(1)} %slice_reduce_fusion.7) | copy-start | bytes 388 | tf_op jit(solution)/shard_map/while
  493.8 34.3 %copy-start.14 = (f32[32,256]{1,0:T(8,128)}, f32[32,256]{1,0:T(8,128)S(1)}, u32[]{:S(2)}) copy-start(f32[32,256]{1,0:T(8,128)S(1)} %get-tuple-element.369) | copy-start | bytes 98308 | tf_op jit(solution)/shard_map/while
  528.1 7.1 copy-start.8
  544.9 12.6 %copy-start.22 = (f32[32]{0:T(128)S(1)}, f32[32]{0:T(128)}, u32[]{:S(2)}) copy-start(f32[32]{0:T(128)} %copy-done.20) | copy-start | bytes 388 | tf_op jit(solution)/shard_map/while
  544.9 17.0 %copy-start.2 = (bf16[1,1,8192,64]{2,3,1,0:T(8,128)(2,1)S(1)}, bf16[1,1,8192,64]{2,3,1,0:T(8,128)(2,1)}, u32[]{:S(2)}) copy-start(bf16[1,1,8192,64]{2,3,1,0:T(8,128)(2,1)} %copy-done.1) | copy-start | bytes 3145732 | tf_op jit(solution)/shard_map/while
  565.1 6.2 copy-start.18
  565.1 6.2 copy-start.26
  565.2 6.2 copy-start.28
  565.2 6.2 copy-start.30
  577.0 20.3 %copy-start.20 = (f32[32]{0:T(128)}, f32[32]{0:T(128)S(1)}, u32[]{:S(2)}) copy-start(f32[32]{0:T(128)S(1)} %slice_reduce_fusion.7) | copy-start | bytes 388 | tf_op jit(solution)/shard_map/while
  598.0 34.3 %copy-start.14 = (f32[32,256]{1,0:T(8,128)}, f32[32,256]{1,0:T(8,128)S(1)}, u32[]{:S(2)}) copy-start(f32[32,256]{1,0:T(8,128)S(1)} %get-tuple-element.369) | copy-start | bytes 98308 | tf_op jit(solution)/shard_map/while
  632.3 7.1 copy-start.8
  649.1 12.6 %copy-start.22 = (f32[32]{0:T(128)S(1)}, f32[32]{0:T(128)}, u32[]{:S(2)}) copy-start(f32[32]{0:T(128)} %copy-done.20) | copy-start | bytes 388 | tf_op jit(solution)/shard_map/while
  649.1 17.0 %copy-start.2 = (bf16[1,1,8192,64]{2,3,1,0:T(8,128)(2,1)S(1)}, bf16[1,1,8192,64]{2,3,1,0:T(8,128)(2,1)}, u32[]{:S(2)}) copy-start(bf16[1,1,8192,64]{2,3,1,0:T(8,128)(2,1)} %copy-done.1) | copy-start | bytes 3145732 | tf_op jit(solution)/shard_map/while
  669.3 6.1 copy-start.18
  669.4 6.1 copy-start.26
  669.4 6.1 copy-start.28
  669.4 6.1 copy-start.30
  690.8 28.4 %all-to-all-start.6 = ((bf16[32,2,512]{2,1,0:T(2,128)(2,1)}), bf16[32,2,512]{2,1,0:T(2,128)(2,1)S(1)}, u32[]{:S(2)}, u32[]{:S(2)}) async-start(bf16[32,2,512]{2,1,0:T(2,128)(2,1)} %reshape.1320), calls=%async_computation.6 | async-start | bytes 131072 | tf_op jit(solution)/shard_map/all_to_all | solution.py:172
  719.2 59.0 %all-to-all-start.4 = ((bf16[32,2,32768]{2,1,0:T(2,128)(2,1)}), bf16[32,2,32768]{2,1,0:T(2,128)(2,1)}, u32[]{:S(2)}, u32[]{:S(2)}) async-start(bf16[32,2,32768]{2,1,0:T(2,128)(2,1)} %reshape.1318), calls=%async_computation.4 | async-start | bytes 8388608 | tf_op jit(solution)/shard_map/all_to_all | solution.py:171
  756.7 30.9 %copy-start.24 = (f32[4,1,3]{2,1,0:T(1,128)S(1)}, f32[4,1,3]{2,1,0:T(1,128)}, u32[]{:S(2)}) copy-start(f32[4,1,3]{2,1,0:T(1,128)} %get-tuple-element.497) | copy-start | bytes 148
  778.2 142.8 %all-to-all-start.5 = ((f32[8192,1,256]{2,1,0:T(1,128)}), f32[8192,1,256]{2,1,0:T(1,128)}, u32[]{:S(2)}, u32[]{:S(2)}) async-start(f32[8192,1,256]{2,1,0:T(1,128)} %reshape.1288), calls=%async_computation.5 | async-start | bytes 16777216 | tf_op jit(solution)/shard_map/all_to_all | solution.py:177
  (68 other events, 244.1 us)
where the time goes:
time: 940 us; the launch traced here: 929 us
  local copies, waits for them, and re-layouts  248 us (26%)
  matrix products  201 us (21%)
  waiting for transfers between devices  174 us (19%)
  other arithmetic  130 us (14%)
  blocking collectives  76.5 us (8%)
  starting transfers between devices  62 us (7%)
  loops' own time  36.8 us (4%)
    unnamed x29, local copies, waits for them, and re-layouts  82.6 us
    psum x1, blocking collectives, body(): head_gradients = lax.psum(grad_params.T, 'dp') * factor  76.5 us
    dot_general x12, matrix products, spanned_scan(): jnp.einsum('cin,cjn->cij', read_blk, write_blk, preferred_element_type=FL)  72.8 us
    all_to_all x1, waiting for transfers between devices, body(): lax.all_to_all(grad_rows, 'seq', split_axis=1, concat_axis=0, tiled=True)  54.5 us
    all_to_all x1, waiting for transfers between devices, body(): lax.all_to_all(proj_rows, 'seq', split_axis=1, concat_axis=0, tiled=True)  48.9 us
    all_to_all x1, waiting for transfers between devices, body(): lax.all_to_all(input_rows, 'seq', split_axis=1, concat_axis=0, tiled=True)  48.9 us
    dynamic_update_slice x16, other arithmetic, over_heads(): result = lax.map(lambda group_args: jax.vmap(function)(*group_args), shaped)  45.6 us
    dot_general x12, matrix products, spanned_scan(): jnp.einsum('cjn,cjp->cpn', scaled_writes, input_blk, preferred_element_ty...  44.5 us
  transfers between devices with their start and end apart: 7, of which 4 were waited for; matrix products, arithmetic and copies ran while one was open for 16% of the time, Pallas kernels for 0%

commit v1 on v0

v1 whole, which is shorter than its diff:
```python
import functools
import math

import jax
import jax.numpy as jnp
from jax import lax
from jax.experimental import pallas as pl
from jax.experimental.pallas import tpu as pltpu
from jax.sharding import PartitionSpec as P

HEADDIM = 64
NSTATE = 128
BLOCK = 256
HALF = 128
PER_GROUP = 16
PAIRS = 8
GW = PER_GROUP * HEADDIM
MSG = 4 * 128 + 16

BF = jnp.bfloat16
FL = jnp.float32


def dot(a, b):
    return jnp.dot(a, b, preferred_element_type=FL)


def dot_nt(a, b):
    return lax.dot_general(a, b, (((1,), (1,)), ((), ())), preferred_element_type=FL)


def dot_tn(a, b):
    return lax.dot_general(a, b, (((0,), (0,)), ((), ())), preferred_element_type=FL)


def hi_lo(a):
    hi = a.astype(BF)
    return hi, (a - hi.astype(FL)).astype(BF)


def three(a):
    hi, _ = hi_lo(a)
    rest = a - hi.astype(FL)
    mid, low = hi_lo(rest)
    return hi, mid, low


def cat_hi_lo(a):
    return jnp.concatenate(hi_lo(a), axis=1)


def tri_sum(tri, a):
    hi, mid, low = three(a)
    return dot(tri, hi) + dot(tri, mid) + dot(tri, low)


def triangle(upper):
    row = lax.broadcasted_iota(jnp.int32, (BLOCK, BLOCK), 0)
    col = lax.broadcasted_iota(jnp.int32, (BLOCK, BLOCK), 1)
    keep = (col >= row) if upper else (col <= row)
    return jnp.where(keep, 1.0, 0.0).astype(BF)


def spread(g, heads, copies):
    row = lax.broadcasted_iota(jnp.int32, (copies * heads, GW), 0)
    col = lax.broadcasted_iota(jnp.int32, (copies * heads, GW), 1)
    if copies == 2:
        row = jnp.where(row >= heads, row - heads, row)
    return jnp.where(row == g * PER_GROUP + col // HEADDIM, 1.0, 0.0).astype(BF)


def gather_heads(p, sel):
    hi, lo = hi_lo(p)
    return dot_nt(hi, sel) + dot_nt(lo, sel)


def rates(raw, prm):
    v = raw.astype(FL) + prm[0:1]
    e = jnp.exp(-jnp.abs(v))
    small = e * (1.0 - e * (0.5 - e * (1.0 / 3 - e * (0.25 - e * 0.2))))
    step = jnp.maximum(v, 0.0) + jnp.where(e < 0.03125, small, jnp.log(1.0 + e))
    rate = -jnp.exp(prm[1:2])
    decay = rate * step
    within = tri_sum(triangle(False), decay)
    return v, step, rate, decay, within


def phase_one(g, heads, x_ref, dy_ref, w_ref, r_ref, cat_te, cat_ew, last3, sd_ref):
    lanes = pl.ds(pl.multiple_of(g * GW, GW), GW)
    glanes = pl.ds(pl.multiple_of(g * NSTATE, NSTATE), NSTATE)
    sel2 = spread(g, heads, 2)
    xt = (x_ref[:, lanes].astype(FL) * dot(cat_te, sel2)).astype(BF)
    dyw = (dy_ref[:, lanes].astype(FL) * dot(cat_ew, sel2)).astype(BF)
    state = dot_tn(w_ref[:, glanes], xt).astype(BF)
    dcar = dot_tn(r_ref[:, glanes], dyw).astype(BF)
    lx = dot(last3, sel2[:heads]).astype(BF)
    for p in range(PAIRS):
        o, slot = g * (PAIRS // 2) + p // 2, p % 2
        sl = slice(p * 128, p * 128 + 128)
        sd_ref[o, slot * 128 : slot * 128 + 128, :] = state[:, sl]
        sd_ref[o, 256 + slot * 128 : 384 + slot * 128, :] = dcar[:, sl]
    for q in range(PAIRS // 2):
        both = jnp.concatenate([lx[:, q * 256 : q * 256 + 128], lx[:, q * 256 + 128 : q * 256 + 256]], axis=0)
        sd_ref[g * (PAIRS // 2) + q, 512:528, :] = both


def decay_factors(step, within):
    last = within[BLOCK - 1 : BLOCK]
    mid = within[HALF - 1 : HALF]
    to_end = jnp.exp(last - within) * step
    from_start = jnp.exp(within)
    to_mid = jnp.exp(mid - within[:HALF]) * step[:HALF]
    from_mid = jnp.exp(within[HALF:] - mid)
    return last, to_end, from_start, to_mid, from_mid


def last_terms(last):
    h, m, l = three(last)
    return jnp.concatenate([h, m, l, jnp.zeros((5, last.shape[1]), BF)], axis=0)


def kernel_a(heads, groups, x_ref, dy_ref, w_ref, r_ref, raw_ref, prm_ref, sd_ref, te_s, ew_s, l3_s):
    _, step, _, _, within = rates(raw_ref[...], prm_ref[...])
    last, to_end, from_start, _, _ = decay_factors(step, within)
    te_s[...] = cat_hi_lo(to_end)
    ew_s[...] = cat_hi_lo(from_start)
    l3_s[...] = last_terms(last)

    def group(g, _):
        phase_one(g, heads, x_ref, dy_ref, w_ref, r_ref, te_s[...], ew_s[...], l3_s[...], sd_ref)
        return 0

    lax.fori_loop(0, groups, group, 0)


def source_decay(m, d, slot):
    rows = m[d, 512 + 8 * slot : 520 + 8 * slot, :].astype(FL)
    return jnp.exp(rows[0:1] + rows[1:2] + rows[2:3])


def kernel_s(blocks, m_ref, back_ref, cf, gf):
    cf[...] = jnp.zeros_like(cf)
    gf[...] = jnp.zeros_like(gf)

    def scan(i, _):
        for slot in range(2):
            rows = slice(slot * 128, slot * 128 + 128)
            back_ref[i, rows, :] = cf[rows, :].astype(BF)
            cf[rows, :] = cf[rows, :] * source_decay(m_ref, i, slot) + m_ref[i, rows, :].astype(FL)
            d = blocks - 1 - i
            rev = slice(256 + slot * 128, 384 + slot * 128)
            back_ref[d, rev, :] = gf[rows, :].astype(BF)
            gf[rows, :] = gf[rows, :] * source_decay(m_ref, d, slot) + m_ref[d, rev, :].astype(FL)
        return 0

    lax.fori_loop(0, blocks, scan, 0)


def intra(g, heads, x_ref, dy_ref, w_ref, r_ref, within, wt_s, st_s, cat_tm, cat_fm, dxa, pr, pc, sel2):
    lanes = pl.ds(pl.multiple_of(g * GW, GW), GW)
    glanes = pl.ds(pl.multiple_of(g * NSTATE, NSTATE), NSTATE)
    wg, rg = w_ref[:, glanes], r_ref[:, glanes]
    row = lax.broadcasted_iota(jnp.int32, (HALF, HALF), 0)
    col = lax.broadcasted_iota(jnp.int32, (HALF, HALF), 1)
    lower = col <= row
    first = lax.broadcasted_iota(jnp.int32, (HALF, 128), 1) < HEADDIM
    scores = dot_nt(rg, wg)
    tm = dot(cat_tm, sel2)
    x0 = x_ref[:HALF, lanes].astype(FL)
    xt1 = (x0 * tm).astype(BF)
    dy1 = (dy_ref[HALF:, lanes].astype(FL) * dot(cat_fm, sel2)).astype(BF)
    sb = scores[HALF:, :HALF].astype(BF)
    z = dot(sb, xt1)
    yb = dot_tn(sb, dy1)
    ds_low = dot_nt(dy1, xt1)
    pr[:HALF, :] = jnp.zeros((HALF, GW), FL)
    pr[HALF:, :] = dy1.astype(FL) * z
    pc[:HALF, :] = xt1.astype(FL) * yb
    pc[HALF:, :] = jnp.zeros((HALF, GW), FL)
    dxa[:HALF, lanes] = tm * yb
    dxa[HALF:, lanes] = jnp.zeros((HALF, GW), FL)
    wr = pltpu.roll(within, lax.rem(heads - g * PER_GROUP, heads), 1)
    wt = wt_s[pl.ds(pl.multiple_of(g * PER_GROUP, PER_GROUP), PER_GROUP), :]
    st = st_s[pl.ds(pl.multiple_of(g * PER_GROUP, PER_GROUP), PER_GROUP), :]
    ds_diag = []
    for sub in range(2):
        rs = slice(sub * HALF, sub * HALF + HALF)
        sd = jnp.where(lower, scores[rs, rs], 0.0)
        ds = jnp.zeros((HALF, HALF), FL)
        for p in range(PAIRS):
            pls = pl.ds(pl.multiple_of(g * GW + p * 128, 128), 128)
            here = slice(p * 128, p * 128 + 128)
            xp, dyp = x_ref[rs, pls], dy_ref[rs, pls]
            none = jnp.zeros_like(xp)
            xst = jnp.concatenate([jnp.where(first, xp, none), jnp.where(first, none, xp)], axis=0)
            dyst = jnp.concatenate([jnp.where(first, dyp, none), jnp.where(first, none, dyp)], axis=0)
            dw = dot_nt(dyp, xst)
            parts = []
            for k in range(2):
                h = 2 * p + k
                gap = jnp.minimum(wr[rs, h : h + 1] - wt[h : h + 1, rs], 0.0)
                es = jnp.exp(gap) * st[h : h + 1, rs]
                ds += dw[:, k * HALF : k * HALF + HALF] * es
                parts.append((sd * es).astype(BF))
            y = dot(jnp.concatenate(parts, axis=1), xst)
            dxp = dot_tn(jnp.concatenate(parts, axis=0), dyst)
            pr[rs, here] += dyp.astype(FL) * y
            pc[rs, here] += xp.astype(FL) * dxp
            dxa[rs, pls] += dxp
        ds_diag.append(jnp.where(lower, ds, 0.0))
    top = jnp.concatenate([ds_diag[0], jnp.zeros((HALF, HALF), FL)], axis=1)
    low = jnp.concatenate([ds_low, ds_diag[1]], axis=1)
    dscore = jnp.concatenate([top, low], axis=0).astype(BF)
    return dot(dscore, wg), dot_tn(dscore, rg)


def kernel_b(
    heads, groups, x_ref, dy_ref, w_ref, r_ref, raw_ref, prm_ref, sd_ref, cg_ref,
    dx_ref, dw_ref, dr_ref, dstep_ref, hg_ref,
    within_s, step_s, wt_s, st_s, te_s, ew_s, tm_s, fm_s, r_acc, c_acc, dl_acc, sk_acc, dxa, pr, pc,
):
    _, step, _, _, within = rates(raw_ref[...], prm_ref[...])
    last, to_end, from_start, to_mid, from_mid = decay_factors(step, within)
    within_s[...] = within
    step_s[...] = step
    wt_s[...] = within.T
    st_s[...] = step.T
    te_s[...] = cat_hi_lo(to_end)
    ew_s[...] = cat_hi_lo(from_start)
    tm_s[...] = cat_hi_lo(to_mid)
    fm_s[...] = cat_hi_lo(from_mid)
    for acc in (r_acc, c_acc, dl_acc, sk_acc):
        acc[...] = jnp.zeros_like(acc)
    full = jnp.concatenate([jnp.exp(last), prm_ref[2:3], jnp.zeros((6, heads), FL)], axis=0)
    full = cat_hi_lo(full)

    def group(g, _):
        lanes = pl.ds(pl.multiple_of(g * GW, GW), GW)
        glanes = pl.ds(pl.multiple_of(g * NSTATE, NSTATE), NSTATE)
        sel2 = spread(g, heads, 2)
        sel = sel2[:heads]
        dr_i, dw_i = intra(g, heads, x_ref, dy_ref, w_ref, r_ref, within_s[...], wt_s, st_s, tm_s[...], fm_s[...], dxa, pr, pc, sel2)
        xf, dyf = x_ref[:, lanes].astype(FL), dy_ref[:, lanes].astype(FL)
        te = dot(te_s[...], sel2)
        xt = (xf * te).astype(BF)
        dyw = (dyf * dot(ew_s[...], sel2)).astype(BF)
        wide = dot(full, sel2)
        g4 = g * (PAIRS // 2)

        def lane_cat(ref, base):
            return jnp.concatenate(
                [ref[g4 + p // 2, base + (p % 2) * 128 : base + (p % 2) * 128 + 128, :] for p in range(PAIRS)], axis=1
            )

        car, gst, own = lane_cat(cg_ref, 0), lane_cat(cg_ref, 256), lane_cat(sd_ref, 0)
        zc = dot(r_ref[:, glanes], car)
        zg = dot(w_ref[:, glanes], gst)
        pr[...] += dyw.astype(FL) * zc
        pc[...] += xt.astype(FL) * zg
        r_acc[...] += gather_heads(pr[...], sel)
        c_acc[...] += gather_heads(pc[...], sel)
        ends = jnp.sum(gst.astype(FL) * (own.astype(FL) + wide[0:1] * car.astype(FL)), axis=0, keepdims=True)
        skips = jnp.sum(xf * dyf, axis=0, keepdims=True)
        both = jnp.concatenate([ends, skips, jnp.zeros((6, GW), FL)], axis=0)
        both = gather_heads(both, sel)
        dl_acc[...] += both[0:1]
        sk_acc[...] += both[1:2]
        dx_ref[:, lanes] = (dxa[:, lanes] + te * zg + wide[1:2] * dyf).astype(BF)
        dr_ref[:, glanes] = (dr_i + dot_nt(dyw, car)).astype(BF)
        dw_ref[:, glanes] = (dw_i + dot_nt(xt, gst)).astype(BF)
        return 0

    lax.fori_loop(0, groups, group, 0)
    v, step, rate, decay, _ = rates(raw_ref[...], prm_ref[...])
    trow = lax.broadcasted_iota(jnp.int32, (BLOCK, heads), 0)
    dwithin = r_acc[...] - c_acc[...] + jnp.where(trow == BLOCK - 1, dl_acc[...], 0.0)
    dld = tri_sum(triangle(True), dwithin)
    dstep = c_acc[...] / step + rate * dld
    draw = dstep / (1.0 + jnp.exp(-v))
    dstep_ref[...] = draw.astype(BF)
    hg_ref[...] = jnp.concatenate(
        [
            jnp.sum(dld * decay, axis=0, keepdims=True),
            jnp.sum(draw, axis=0, keepdims=True),
            sk_acc[...],
            jnp.zeros((5, heads), FL),
        ],
        axis=0,
    )


def body(head_inputs, write_proj, read_projection, step_raw, output_grad, decay_log, step_bias, skip_gain):
    n = lax.axis_size("seq")
    x, w, r, raw, dy = head_inputs[0], write_proj[0], read_projection[0], step_raw[0], output_grad[0]
    heads = raw.shape[1]
    groups = heads // PER_GROUP
    owned = heads // n
    factor = 1.0 / math.sqrt(lax.axis_size("dp") * n * BLOCK * HEADDIM)
    prm = jnp.stack([step_bias, decay_log, skip_gain])
    prm = lax.all_gather(prm, "seq", axis=1, tiled=True)
    prm = jnp.concatenate([prm, jnp.zeros((5, heads), FL)], axis=0)
    vm = pl.BlockSpec(memory_space=pltpu.VMEM)
    params = pltpu.CompilerParams(vmem_limit_bytes=60 * 2**20)
    cat2 = pltpu.VMEM((BLOCK, 2 * heads), BF)
    cat1 = pltpu.VMEM((HALF, 2 * heads), BF)
    sd = pl.pallas_call(
        functools.partial(kernel_a, heads, groups),
        out_shape=jax.ShapeDtypeStruct((n, MSG, 128), BF),
        in_specs=[vm] * 6,
        out_specs=vm,
        scratch_shapes=[cat2, cat2, pltpu.VMEM((8, heads), BF)],
        compiler_params=params,
        name="block_states",
    )(x, dy, w, r, raw, prm)
    got = lax.all_to_all(sd, "seq", split_axis=0, concat_axis=0, tiled=True)
    back = pl.pallas_call(
        functools.partial(kernel_s, n),
        out_shape=jax.ShapeDtypeStruct((n, 512, 128), BF),
        in_specs=[vm],
        out_specs=vm,
        scratch_shapes=[pltpu.VMEM((256, 128), FL)] * 2,
        compiler_params=params,
        name="state_scan",
    )(got)
    cg = lax.all_to_all(back, "seq", split_axis=0, concat_axis=0, tiled=True)
    full = pltpu.VMEM((BLOCK, heads), FL)
    tr = pltpu.VMEM((heads, BLOCK), FL)
    row = pltpu.VMEM((1, heads), FL)
    wide = pltpu.VMEM((BLOCK, GW), FL)
    dx, dw, dr, dstep, hg = pl.pallas_call(
        functools.partial(kernel_b, heads, groups),
        out_shape=[
            jax.ShapeDtypeStruct(x.shape, BF),
            jax.ShapeDtypeStruct(w.shape, BF),
            jax.ShapeDtypeStruct(r.shape, BF),
            jax.ShapeDtypeStruct(raw.shape, BF),
            jax.ShapeDtypeStruct((8, heads), FL),
        ],
        in_specs=[vm] * 8,
        out_specs=[vm] * 5,
        scratch_shapes=[full, full, tr, tr, cat2, cat2, cat1, cat1, full, full, row, row,
                        pltpu.VMEM((BLOCK, heads * HEADDIM), FL), wide, wide],
        compiler_params=params,
        name="gradients",
    )(x, dy, w, r, raw, prm, sd, cg)
    hg = lax.psum(hg, ("dp", "seq"))
    hg = lax.dynamic_slice_in_dim(hg[:3], lax.axis_index("seq") * owned, owned, 1) * factor
    return (dx[None], dw[None], dr[None], dstep[None], hg)


def solution(mesh):
    tok = P("dp", "seq", None)
    return jax.shard_map(
        body,
        mesh=mesh,
        in_specs=(tok, tok, tok, tok, tok, P("seq"), P("seq"), P("seq")),
        out_specs=(tok, tok, tok, tok, P(None, "seq")),
        check_vma=False,
    )
```

time: 940 us -> 306 us (0.33)
  the two profiles are of different devices: /device:TPU:54 before, /device:TPU:1 now
where the time goes in v1:
time: 306 us
  blocking collectives  193 us (63%)
  Pallas kernels  63.4 us (21%)
  waiting for transfers between devices  41 us (13%)
  starting transfers between devices  5.25 us (2%)
    psum x1, blocking collectives, body(): hg = lax.psum(hg, ('dp', 'seq'))  80.6 us
    all_gather x1, blocking collectives, body(): prm = lax.all_gather(prm, 'seq', axis=1, tiled=True)  68.7 us
    pallas_call x1, Pallas kernels, body(): pl.pallas_call(functools.partial(kernel_b, heads, groups), out_shape=[jax...  45.8 us
    all_to_all x1, blocking collectives, body(): got = lax.all_to_all(sd, 'seq', split_axis=0, concat_axis=0, tiled=True)  44.1 us
    all_to_all x1, waiting for transfers between devices, body(): cg = lax.all_to_all(back, 'seq', split_axis=0, concat_axis=0, tiled=True)  41 us
    pallas_call x1, Pallas kernels, body(): pl.pallas_call(functools.partial(kernel_a, heads, groups), out_shape=jax....  11.5 us
  transfers between devices with their start and end apart: 1, of which 1 were waited for; matrix products, arithmetic and copies ran while one was open for 0% of the time, Pallas kernels for 0%

profile of v1, /device:TPU:1, one launch (start us, length us, event | category | flops | bytes accessed | tf_op | source)
XLA Modules:
  0.0 305.8 jit_solution(15997622990639425957)
XLA Ops:
  0.6 0.7 maximum_bitcast_fusion
  1.3 0.1 copy.17
  1.4 68.7 %all-gather = f32[32,4,3]{2,1,0:T(4,128)S(1)} all-gather(f32[1,4,3]{2,1,0:T(4,128)S(1)} %bitcast.29), channel_id=1, replica_groups=mesh['dp'=4,'seq'=32] {'seq'}, dimensions={0}, use_global_device_ids=true | all-gather | bytes 1584 | tf_op jit(solution)/shard_map/all_gather | solution.py:300
  70.2 0.1 copy.19
  70.2 0.6 concatenate.3.prm_ref
  70.8 11.5 %block_states.1.sd_ref = bf16[32,528,128]{2,1,0:T(8,128)(2,1)} custom-call(bf16[256,8192]{1,0:T(8,128)(2,1)} %bitcast.17, bf16[256,8192]{1,0:T(8,128)(2,1)} %bitcast.19, bf16[256,1024]{1,0:T(8,128)(2,1)} %bitcast.21, bf16[256,1024]{1,0:T(8,128)(2,1)} %bitcast.23, bf16[256,128]{1,0:T(8,128)(2,1)} %bitcast.25, f32[8,128]{1,0:T(8,128)} %concatenate.3.prm_ref), custom_call_target="tpu_custom_call" | custom-call | tf_op jit(solution)/shard_map/block_states/pallas_call | solution.py:306
  82.3 44.1 %all_to_all.10.m_ref = bf16[32,528,128]{2,1,0:T(8,128)(2,1)} all-to-all(bf16[32,528,128]{2,1,0:T(8,128)(2,1)} %block_states.1.sd_ref), channel_id=1, replica_groups=mesh['dp'=4,'seq'=32] {'seq'}, dimensions={0} | all-to-all | bytes 8650752 | tf_op jit(solution)/shard_map/all_to_all | solution.py:315
  126.4 6.1 %state_scan.1 = bf16[32,512,128]{2,1,0:T(8,128)(2,1)} custom-call(bf16[32,528,128]{2,1,0:T(8,128)(2,1)} %all_to_all.10.m_ref), custom_call_target="tpu_custom_call" | custom-call | tf_op jit(solution)/shard_map/state_scan/pallas_call | solution.py:316
  132.6 5.3 %all-to-all-start.1 = ((bf16[32,512,128]{2,1,0:T(8,128)(2,1)}), bf16[32,512,128]{2,1,0:T(8,128)(2,1)}, u32[]{:S(2)}, u32[]{:S(2)}) async-start(bf16[32,512,128]{2,1,0:T(8,128)(2,1)} %state_scan.1), calls=%async_computation.1 | async-start | bytes 8388608 | tf_op jit(solution)/shard_map/all_to_all | solution.py:325
  137.8 41.0 %all-to-all-done.1.cg_ref = bf16[32,512,128]{2,1,0:T(8,128)(2,1)} async-done(((bf16[32,512,128]{2,1,0:T(8,128)(2,1)}), bf16[32,512,128]{2,1,0:T(8,128)(2,1)}, u32[]{:S(2)}, u32[]{:S(2)}) %all-to-all-start.1) | async-done | bytes 4194336 | tf_op jit(solution)/shard_map/all_to_all | solution.py:325
  178.8 45.8 %gradients.1 = (bf16[256,8192]{1,0:T(8,128)(2,1)}, bf16[256,1024]{1,0:T(8,128)(2,1)}, bf16[256,1024]{1,0:T(8,128)(2,1)}, bf16[256,128]{1,0:T(8,128)(2,1)}, f32[8,128]{1,0:T(8,128)}) custom-call(bf16[256,8192]{1,0:T(8,128)(2,1)} %bitcast.18, bf16[256,8192]{1,0:T(8,128)(2,1)} %bitcast.20, bf16[256,1024]{1,0:T(8,128)(2,1)} %bitcast.22, ...), custom_call_target="tpu_custom_call" | custom-call | tf_op jit(solution)/shard_map/gradients/pallas_call | solution.py:330
  224.6 80.6 %psum.7 = f32[8,128]{1,0:T(8,128)S(1)} all-reduce(f32[8,128]{1,0:T(8,128)} %get-tuple-element.14), channel_id=1, replica_groups=mesh['dp'=4,'seq'=32] {'dp','seq'}, use_global_device_ids=true, to_apply=%region_0.0 | all-reduce | flops 1024 | bytes 8192 | tf_op jit(solution)/shard_map/psum | solution.py:346
  305.2 0.7 dynamic-slice_multiply_fusion
  (1 shorter events, 0.0 us)
Async XLA Ops:
  132.6 46.2 %all-to-all-start.1 = ((bf16[32,512,128]{2,1,0:T(8,128)(2,1)}), bf16[32,512,128]{2,1,0:T(8,128)(2,1)}, u32[]{:S(2)}, u32[]{:S(2)}) async-start(bf16[32,512,128]{2,1,0:T(8,128)(2,1)} %state_scan.1), calls=%async_computation.1 | async-start | bytes 8388608 | tf_op jit(solution)/shard_map/all_to_all | solution.py:325

commit v2 on v1

--- a/solution.py
+++ b/solution.py
@@ -19,6 +19,7 @@
 
 BF = jnp.bfloat16
 FL = jnp.float32
+MESH = pl.DeviceIdType.MESH
 
 
 def dot(a, b):
@@ -119,41 +120,9 @@
     return jnp.concatenate([h, m, l, jnp.zeros((5, last.shape[1]), BF)], axis=0)
 
 
-def kernel_a(heads, groups, x_ref, dy_ref, w_ref, r_ref, raw_ref, prm_ref, sd_ref, te_s, ew_s, l3_s):
-    _, step, _, _, within = rates(raw_ref[...], prm_ref[...])
-    last, to_end, from_start, _, _ = decay_factors(step, within)
-    te_s[...] = cat_hi_lo(to_end)
-    ew_s[...] = cat_hi_lo(from_start)
-    l3_s[...] = last_terms(last)
-
-    def group(g, _):
-        phase_one(g, heads, x_ref, dy_ref, w_ref, r_ref, te_s[...], ew_s[...], l3_s[...], sd_ref)
-        return 0
-
-    lax.fori_loop(0, groups, group, 0)
-
-
 def source_decay(m, d, slot):
     rows = m[d, 512 + 8 * slot : 520 + 8 * slot, :].astype(FL)
     return jnp.exp(rows[0:1] + rows[1:2] + rows[2:3])
-
-
-def kernel_s(blocks, m_ref, back_ref, cf, gf):
-    cf[...] = jnp.zeros_like(cf)
-    gf[...] = jnp.zeros_like(gf)
-
-    def scan(i, _):
-        for slot in range(2):
-            rows = slice(slot * 128, slot * 128 + 128)
-            back_ref[i, rows, :] = cf[rows, :].astype(BF)
-            cf[rows, :] = cf[rows, :] * source_decay(m_ref, i, slot) + m_ref[i, rows, :].astype(FL)
-            d = blocks - 1 - i
-            rev = slice(256 + slot * 128, 384 + slot * 128)
-            back_ref[d, rev, :] = gf[rows, :].astype(BF)
-            gf[rows, :] = gf[rows, :] * source_decay(m_ref, d, slot) + m_ref[d, rev, :].astype(FL)
-        return 0
-
-    lax.fori_loop(0, blocks, scan, 0)
 
 
 def intra(g, heads, x_ref, dy_ref, w_ref, r_ref, within, wt_s, st_s, cat_tm, cat_fm, dxa, pr, pc, sel2):
@@ -214,71 +183,226 @@
     return dot(dscore, wg), dot_tn(dscore, rg)
 
 
-def kernel_b(
-    heads, groups, x_ref, dy_ref, w_ref, r_ref, raw_ref, prm_ref, sd_ref, cg_ref,
-    dx_ref, dw_ref, dr_ref, dstep_ref, hg_ref,
-    within_s, step_s, wt_s, st_s, te_s, ew_s, tm_s, fm_s, r_acc, c_acc, dl_acc, sk_acc, dxa, pr, pc,
+def kernel(
+    heads, groups, n, dps, factor,
+    x_hbm, dy_hbm, w_hbm, r_hbm, raw_ref, bias_ref, dlog_ref, gain_ref,
+    dx_hbm, dw_ref, dr_ref, dstep_ref, hg_ref,
+    x_ref, dy_ref, w_ref, r_ref, prm_s, within_s, wt_s, st_s, te_s, ew_s, tm_s, fm_s, l3_s, full_s,
+    r_acc, c_acc, dl_acc, sk_acc, dxa, pr, pc, dri, dwi, dxo,
+    pg, sd, got, back, cg, cf, hb, hd,
+    in_sem, out_sem, pg_s, pg_r, s1, r1, s2, r2, hb_s, hb_r, hd_s, hd_r,
 ):
-    _, step, _, _, within = rates(raw_ref[...], prm_ref[...])
+    c = lax.axis_index("seq")
+    d = lax.axis_index("dp")
+    per = PAIRS // 2
+    home = c // per
+    loads = [
+        pltpu.make_async_copy(a, b, in_sem.at[i])
+        for i, (a, b) in enumerate(((x_hbm, x_ref), (dy_hbm, dy_ref), (w_hbm, w_ref), (r_hbm, r_ref)))
+    ]
+    for load in loads:
+        load.start()
+
+    barrier = pltpu.get_barrier_semaphore()
+
+    def greet(i, _):
+        pl.semaphore_signal(barrier, inc=1, device_id={"seq": lax.rem(c + i, n)}, device_id_type=MESH)
+        return 0
+
+    lax.fori_loop(1, n, greet, 0)
+    for i in range(1, dps):
+        pl.semaphore_signal(barrier, inc=1, device_id={"dp": lax.rem(d + i, dps)}, device_id_type=MESH)
+    pl.semaphore_wait(barrier, n - 1 + dps - 1)
+
+    lane = lax.broadcasted_iota(jnp.int32, (8, heads), 1)
+    prow = lax.broadcasted_iota(jnp.int32, (8, heads), 0)
+    mine = jnp.zeros((8, heads), FL)
+    owned = heads // n
+    for row, ref in enumerate((bias_ref, dlog_ref, gain_ref)):
+        for k in range(owned):
+            mine = jnp.where((prow == row) & (lane == c * owned + k), ref[k], mine)
+    pg[c] = mine
+
+    def to_all(buf, send, recv, wait):
+        def one(t):
+            return pltpu.make_async_remote_copy(
+                src_ref=buf.at[c], dst_ref=buf.at[c], send_sem=send.at[t], recv_sem=recv.at[c],
+                device_id={"seq": t}, device_id_type=MESH,
+            )
+
+        def other(t):
+            return pltpu.make_async_remote_copy(
+                src_ref=buf.at[t], dst_ref=buf.at[t], send_sem=send.at[t], recv_sem=recv.at[t],
+                device_id={"seq": t}, device_id_type=MESH,
+            )
+
+        def step(i, _):
+            t = lax.rem(c + i, n)
+            if wait:
+                one(t).wait_send()
+                other(t).wait_recv()
+            else:
+                one(t).start()
+            return 0
+
+        lax.fori_loop(1, n, step, 0)
+
+    to_all(pg, pg_s, pg_r, False)
+    for acc in (r_acc, c_acc, dl_acc, sk_acc):
+        acc[...] = jnp.zeros_like(acc)
+    to_all(pg, pg_s, pg_r, True)
+    prm_s[...] = jnp.sum(pg[...], axis=0)
+    _, step, _, _, within = rates(raw_ref[...], prm_s[...])
     last, to_end, from_start, to_mid, from_mid = decay_factors(step, within)
     within_s[...] = within
-    step_s[...] = step
     wt_s[...] = within.T
     st_s[...] = step.T
     te_s[...] = cat_hi_lo(to_end)
     ew_s[...] = cat_hi_lo(from_start)
     tm_s[...] = cat_hi_lo(to_mid)
     fm_s[...] = cat_hi_lo(from_mid)
-    for acc in (r_acc, c_acc, dl_acc, sk_acc):
-        acc[...] = jnp.zeros_like(acc)
-    full = jnp.concatenate([jnp.exp(last), prm_ref[2:3], jnp.zeros((6, heads), FL)], axis=0)
-    full = cat_hi_lo(full)
-
-    def group(g, _):
+    l3_s[...] = last_terms(last)
+    full_s[...] = cat_hi_lo(jnp.concatenate([jnp.exp(last), prm_s[2:3], jnp.zeros((6, heads), FL)], axis=0))
+    for load in loads:
+        load.wait()
+
+    def out(o):
+        return pltpu.make_async_remote_copy(
+            src_ref=sd.at[o], dst_ref=got.at[c], send_sem=s1.at[o], recv_sem=r1.at[c],
+            device_id={"seq": o}, device_id_type=MESH,
+        )
+
+    def out_from(t):
+        return pltpu.make_async_remote_copy(
+            src_ref=sd.at[t], dst_ref=got.at[t], send_sem=s1.at[t], recv_sem=r1.at[t],
+            device_id={"seq": t}, device_id_type=MESH,
+        )
+
+    def states(i, _):
+        g = lax.rem(home + i, groups)
+        phase_one(g, heads, x_ref, dy_ref, w_ref, r_ref, te_s[...], ew_s[...], l3_s[...], sd)
+        for q in range(per):
+            o = g * per + lax.rem(c + q, per)
+
+            @pl.when(o != c)
+            def _():
+                out(o).start()
+
+        return 0
+
+    lax.fori_loop(0, groups, states, 0)
+    got[c] = sd[c]
+
+    def local(g, _):
+        glanes = pl.ds(pl.multiple_of(g * NSTATE, NSTATE), NSTATE)
+        sel2 = spread(g, heads, 2)
+        dr_i, dw_i = intra(
+            g, heads, x_ref, dy_ref, w_ref, r_ref, within_s[...], wt_s, st_s, tm_s[...], fm_s[...], dxa, pr, pc, sel2
+        )
+        dri[:, glanes] = dr_i
+        dwi[:, glanes] = dw_i
+        r_acc[...] += gather_heads(pr[...], sel2[:heads])
+        c_acc[...] += gather_heads(pc[...], sel2[:heads])
+        return 0
+
+    lax.fori_loop(0, groups, local, 0)
+
+    def arrived(i, _):
+        out_from(lax.rem(c + i, n)).wait_recv()
+        return 0
+
+    lax.fori_loop(1, n, arrived, 0)
+
+    def ret(t, half):
+        rows = pl.ds(half * 256, 256)
+        return pltpu.make_async_remote_copy(
+            src_ref=back.at[t, rows], dst_ref=cg.at[c, rows], send_sem=s2.at[half, t], recv_sem=r2.at[half, c],
+            device_id={"seq": t}, device_id_type=MESH,
+        )
+
+    def ret_from(t, half):
+        rows = pl.ds(half * 256, 256)
+        return pltpu.make_async_remote_copy(
+            src_ref=back.at[t, rows], dst_ref=cg.at[t, rows], send_sem=s2.at[half, t], recv_sem=r2.at[half, t],
+            device_id={"seq": t}, device_id_type=MESH,
+        )
+
+    for half in range(2):
+        cf[...] = jnp.zeros_like(cf)
+
+        def scan(i, _):
+            t = i if half == 0 else n - 1 - i
+            for slot in range(2):
+                rows = slice(slot * 128, slot * 128 + 128)
+                mrows = slice(half * 256 + slot * 128, half * 256 + slot * 128 + 128)
+                back[t, mrows, :] = cf[rows, :].astype(BF)
+                cf[rows, :] = cf[rows, :] * source_decay(got, t, slot) + got[t, mrows, :].astype(FL)
+            return 0
+
+        lax.fori_loop(0, n, scan, 0)
+
+        def give(i, _):
+            g = lax.rem(home + i // per, groups)
+            t = g * per + lax.rem(c + i, per)
+
+            @pl.when(t != c)
+            def _():
+                ret(t, half).start()
+
+            return 0
+
+        lax.fori_loop(0, n, give, 0)
+        cg[c, half * 256 : half * 256 + 256, :] = back[c, half * 256 : half * 256 + 256, :]
+
+    def carried(i, _):
+        g = lax.rem(home + groups - i, groups)
+        g4 = g * per
+        for q in range(per):
+            @pl.when(g4 + q != c)
+            def _():
+                ret_from(g4 + q, 0).wait_recv()
+                ret_from(g4 + q, 1).wait_recv()
+
         lanes = pl.ds(pl.multiple_of(g * GW, GW), GW)
         glanes = pl.ds(pl.multiple_of(g * NSTATE, NSTATE), NSTATE)
         sel2 = spread(g, heads, 2)
         sel = sel2[:heads]
-        dr_i, dw_i = intra(g, heads, x_ref, dy_ref, w_ref, r_ref, within_s[...], wt_s, st_s, tm_s[...], fm_s[...], dxa, pr, pc, sel2)
         xf, dyf = x_ref[:, lanes].astype(FL), dy_ref[:, lanes].astype(FL)
         te = dot(te_s[...], sel2)
         xt = (xf * te).astype(BF)
         dyw = (dyf * dot(ew_s[...], sel2)).astype(BF)
-        wide = dot(full, sel2)
-        g4 = g * (PAIRS // 2)
+        wide = dot(full_s[...], sel2)
 
         def lane_cat(ref, base):
             return jnp.concatenate(
                 [ref[g4 + p // 2, base + (p % 2) * 128 : base + (p % 2) * 128 + 128, :] for p in range(PAIRS)], axis=1
             )
 
-        car, gst, own = lane_cat(cg_ref, 0), lane_cat(cg_ref, 256), lane_cat(sd_ref, 0)
+        car, gst, own = lane_cat(cg, 0), lane_cat(cg, 256), lane_cat(sd, 0)
         zc = dot(r_ref[:, glanes], car)
         zg = dot(w_ref[:, glanes], gst)
-        pr[...] += dyw.astype(FL) * zc
-        pc[...] += xt.astype(FL) * zg
-        r_acc[...] += gather_heads(pr[...], sel)
-        c_acc[...] += gather_heads(pc[...], sel)
+        r_acc[...] += gather_heads(dyw.astype(FL) * zc, sel)
+        c_acc[...] += gather_heads(xt.astype(FL) * zg, sel)
         ends = jnp.sum(gst.astype(FL) * (own.astype(FL) + wide[0:1] * car.astype(FL)), axis=0, keepdims=True)
         skips = jnp.sum(xf * dyf, axis=0, keepdims=True)
         both = jnp.concatenate([ends, skips, jnp.zeros((6, GW), FL)], axis=0)
         both = gather_heads(both, sel)
         dl_acc[...] += both[0:1]
         sk_acc[...] += both[1:2]
-        dx_ref[:, lanes] = (dxa[:, lanes] + te * zg + wide[1:2] * dyf).astype(BF)
-        dr_ref[:, glanes] = (dr_i + dot_nt(dyw, car)).astype(BF)
-        dw_ref[:, glanes] = (dw_i + dot_nt(xt, gst)).astype(BF)
-        return 0
-
-    lax.fori_loop(0, groups, group, 0)
-    v, step, rate, decay, _ = rates(raw_ref[...], prm_ref[...])
+        dxo[:, lanes] = (dxa[:, lanes] + te * zg + wide[1:2] * dyf).astype(BF)
+        pltpu.make_async_copy(dxo.at[:, lanes], dx_hbm.at[:, lanes], out_sem.at[g]).start()
+        dr_ref[:, glanes] = (dri[:, glanes] + dot_nt(dyw, car)).astype(BF)
+        dw_ref[:, glanes] = (dwi[:, glanes] + dot_nt(xt, gst)).astype(BF)
+        return 0
+
+    lax.fori_loop(0, groups, carried, 0)
+    v, step, rate, decay, _ = rates(raw_ref[...], prm_s[...])
     trow = lax.broadcasted_iota(jnp.int32, (BLOCK, heads), 0)
     dwithin = r_acc[...] - c_acc[...] + jnp.where(trow == BLOCK - 1, dl_acc[...], 0.0)
     dld = tri_sum(triangle(True), dwithin)
     dstep = c_acc[...] / step + rate * dld
     draw = dstep / (1.0 + jnp.exp(-v))
-    dstep_ref[...] = draw.astype(BF)
-    hg_ref[...] = jnp.concatenate(
+    hb[c] = jnp.concatenate(
         [
             jnp.sum(dld * decay, axis=0, keepdims=True),
             jnp.sum(draw, axis=0, keepdims=True),
@@ -287,48 +411,64 @@
         ],
         axis=0,
     )
+    to_all(hb, hb_s, hb_r, False)
+    dstep_ref[...] = draw.astype(BF)
+    to_all(hb, hb_s, hb_r, True)
+    hd[d] = jnp.sum(hb[...], axis=0)
+
+    def across(j, who):
+        return pltpu.make_async_remote_copy(
+            src_ref=hd.at[who], dst_ref=hd.at[who], send_sem=hd_s.at[j], recv_sem=hd_r.at[who],
+            device_id={"dp": lax.rem(d + j, dps)}, device_id_type=MESH,
+        )
+
+    for j in range(1, dps):
+        across(j, d).start()
+
+    def leave(t, _):
+        @pl.when(t != c)
+        def _():
+            out(t).wait_send()
+            ret(t, 0).wait_send()
+            ret(t, 1).wait_send()
+
+        return 0
+
+    lax.fori_loop(0, n, leave, 0)
+    for j in range(1, dps):
+        across(j, d).wait_send()
+        across(j, lax.rem(d + j, dps)).wait_recv()
+    total = jnp.sum(hd[...], axis=0) * factor
+    hg_ref[...] = pltpu.roll(total, lax.rem(heads - c * owned, heads), 1)
+
+    def written(g, _):
+        lanes = pl.ds(pl.multiple_of(g * GW, GW), GW)
+        pltpu.make_async_copy(dxo.at[:, lanes], dx_hbm.at[:, lanes], out_sem.at[g]).wait()
+        return 0
+
+    lax.fori_loop(0, groups, written, 0)
 
 
 def body(head_inputs, write_proj, read_projection, step_raw, output_grad, decay_log, step_bias, skip_gain):
-    n = lax.axis_size("seq")
+    n, dps = lax.axis_size("seq"), lax.axis_size("dp")
     x, w, r, raw, dy = head_inputs[0], write_proj[0], read_projection[0], step_raw[0], output_grad[0]
     heads = raw.shape[1]
     groups = heads // PER_GROUP
     owned = heads // n
-    factor = 1.0 / math.sqrt(lax.axis_size("dp") * n * BLOCK * HEADDIM)
-    prm = jnp.stack([step_bias, decay_log, skip_gain])
-    prm = lax.all_gather(prm, "seq", axis=1, tiled=True)
-    prm = jnp.concatenate([prm, jnp.zeros((5, heads), FL)], axis=0)
+    factor = 1.0 / math.sqrt(dps * n * BLOCK * HEADDIM)
     vm = pl.BlockSpec(memory_space=pltpu.VMEM)
-    params = pltpu.CompilerParams(vmem_limit_bytes=60 * 2**20)
+    sm = pl.BlockSpec(memory_space=pltpu.SMEM)
+    hbm = pl.BlockSpec(memory_space=pl.ANY)
     cat2 = pltpu.VMEM((BLOCK, 2 * heads), BF)
     cat1 = pltpu.VMEM((HALF, 2 * heads), BF)
-    sd = pl.pallas_call(
-        functools.partial(kernel_a, heads, groups),
-        out_shape=jax.ShapeDtypeStruct((n, MSG, 128), BF),
-        in_specs=[vm] * 6,
-        out_specs=vm,
-        scratch_shapes=[cat2, cat2, pltpu.VMEM((8, heads), BF)],
-        compiler_params=params,
-        name="block_states",
-    )(x, dy, w, r, raw, prm)
-    got = lax.all_to_all(sd, "seq", split_axis=0, concat_axis=0, tiled=True)
-    back = pl.pallas_call(
-        functools.partial(kernel_s, n),
-        out_shape=jax.ShapeDtypeStruct((n, 512, 128), BF),
-        in_specs=[vm],
-        out_specs=vm,
-        scratch_shapes=[pltpu.VMEM((256, 128), FL)] * 2,
-        compiler_params=params,
-        name="state_scan",
-    )(got)
-    cg = lax.all_to_all(back, "seq", split_axis=0, concat_axis=0, tiled=True)
     full = pltpu.VMEM((BLOCK, heads), FL)
     tr = pltpu.VMEM((heads, BLOCK), FL)
     row = pltpu.VMEM((1, heads), FL)
     wide = pltpu.VMEM((BLOCK, GW), FL)
+    small = pltpu.VMEM((n, 8, heads), FL)
+    sem = pltpu.SemaphoreType.DMA
     dx, dw, dr, dstep, hg = pl.pallas_call(
-        functools.partial(kernel_b, heads, groups),
+        functools.partial(kernel, heads, groups, n, dps, factor),
         out_shape=[
             jax.ShapeDtypeStruct(x.shape, BF),
             jax.ShapeDtypeStruct(w.shape, BF),
@@ -336,16 +476,26 @@
             jax.ShapeDtypeStruct(raw.shape, BF),
             jax.ShapeDtypeStruct((8, heads), FL),
         ],
-        in_specs=[vm] * 8,
-        out_specs=[vm] * 5,
-        scratch_shapes=[full, full, tr, tr, cat2, cat2, cat1, cat1, full, full, row, row,
-                        pltpu.VMEM((BLOCK, heads * HEADDIM), FL), wide, wide],
-        compiler_params=params,
-        name="gradients",
-    )(x, dy, w, r, raw, prm, sd, cg)
-    hg = lax.psum(hg, ("dp", "seq"))
-    hg = lax.dynamic_slice_in_dim(hg[:3], lax.axis_index("seq") * owned, owned, 1) * factor
-    return (dx[None], dw[None], dr[None], dstep[None], hg)
+        in_specs=[hbm] * 4 + [vm] + [sm] * 3,
+        out_specs=[hbm] + [vm] * 4,
+        scratch_shapes=[
+            pltpu.VMEM(x.shape, BF), pltpu.VMEM(x.shape, BF), pltpu.VMEM(w.shape, BF), pltpu.VMEM(r.shape, BF),
+            pltpu.VMEM((8, heads), FL), full, tr, tr, cat2, cat2, cat1, cat1,
+            pltpu.VMEM((8, heads), BF), pltpu.VMEM((8, 2 * heads), BF),
+            full, full, row, row,
+            pltpu.VMEM(x.shape, FL), wide, wide, pltpu.VMEM(r.shape, FL), pltpu.VMEM(w.shape, FL), pltpu.VMEM(x.shape, BF),
+            small, pltpu.VMEM((n, MSG, 128), BF), pltpu.VMEM((n, MSG, 128), BF),
+            pltpu.VMEM((n, 512, 128), BF), pltpu.VMEM((n, 512, 128), BF), pltpu.VMEM((256, 128), FL),
+            small, pltpu.VMEM((dps, 8, heads), FL),
+            sem((4,)), sem((groups,)), sem((n,)), sem((n,)), sem((n,)), sem((n,)), sem((2, n)), sem((2, n)),
+            sem((n,)), sem((n,)), sem((dps,)), sem((dps,)),
+        ],
+        compiler_params=pltpu.CompilerParams(
+            collective_id=0, has_side_effects=True, vmem_limit_bytes=60 * 2**20
+        ),
+        name="mixer_backward",
+    )(x, dy, w, r, raw, step_bias, decay_log, skip_gain)
+    return (dx[None], dw[None], dr[None], dstep[None], hg[:3, :owned])
 
 
 def solution(mesh):

time: 306 us -> 185 us (0.60)
  blocking collectives: 193 us -> 0 us
  Pallas kernels: 63.4 us -> 176 us
  waiting for transfers between devices: 41 us -> 0 us
  local copies, waits for them, and re-layouts: 0.77 us -> 8.21 us
  starting transfers between devices: 5.25 us -> 0 us
    pallas_call x3 -> x1, Pallas kernels: 63.4 us -> 176 us  [body(): pl.pallas_call(functools.partial(kernel, heads, groups, n, dps, factor),...]
    psum x1 -> x0, blocking collectives: 80.6 us -> none  [body(): hg = lax.psum(hg, ('dp', 'seq'))]
    all_gather x1 -> x0, blocking collectives: 68.7 us -> none  [body(): prm = lax.all_gather(prm, 'seq', axis=1, tiled=True)]
    all_to_all x1 -> x0, blocking collectives: 44.1 us -> none  [body(): got = lax.all_to_all(sd, 'seq', split_axis=0, concat_axis=0, tiled=True)]
    all_to_all x1 -> x0, waiting for transfers between devices: 41 us -> none  [body(): cg = lax.all_to_all(back, 'seq', split_axis=0, concat_axis=0, tiled=True)]
    unnamed x2 -> x10, local copies, waits for them, and re-layouts: 0.15 us -> 6.96 us
    all_to_all x1 -> x0, starting transfers between devices: 5.25 us -> none  [body(): cg = lax.all_to_all(back, 'seq', split_axis=0, concat_axis=0, tiled=True)]
  transfers between devices with their start and end apart: 1 -> 0, of which waited for: 1 -> 0; matrix products, arithmetic and copies ran while one was open for 0% -> 0% of each run, Pallas kernels for 0% -> 0%
where the time goes in v2:
time: 185 us
  Pallas kernels  176 us (95%)
  local copies, waits for them, and re-layouts  8.21 us (4%)
    pallas_call x1, Pallas kernels, body(): pl.pallas_call(functools.partial(kernel, heads, groups, n, dps, factor),...  176 us
    unnamed x10, local copies, waits for them, and re-layouts  6.96 us

profile of v2, /device:TPU:1, one launch (start us, length us, event | category | flops | bytes accessed | tf_op | source)
XLA Modules:
  0.0 184.8 jit_solution(11172353337630617203)
XLA Ops:
  0.6 176.0 %mixer_backward.1 = (bf16[256,8192]{1,0:T(8,128)(2,1)}, bf16[256,1024]{1,0:T(8,128)(2,1)}, bf16[256,1024]{1,0:T(8,128)(2,1)}, bf16[256,128]{1,0:T(8,128)(2,1)}, f32[8,128]{1,0:T(8,128)}) custom-call(bf16[256,8192]{1,0:T(8,128)(2,1)} %bitcast.9, bf16[256,8192]{1,0:T(8,128)(2,1)} %bitcast.10, bf16[256,1024]{1,0:T(8,128)(2,1)} %bitcast.12, ...), custom_call_target="tpu_custom_call" | custom-call | tf_op jit(solution)/shard_map/mixer_backward/pallas_call | solution.py:470
  176.6 1.2 slice.3
  177.9 0.0 copy-start.1
  177.9 0.0 copy-start
  177.9 0.0 copy-start.2
  177.9 4.7 %copy.17 = bf16[1,256,8192]{2,1,0:T(8,128)(2,1)} copy(bf16[1,256,8192]{2,1,0:T(8,128)(2,1)} %bitcast.11) | data formatting | bytes 8388608
  182.6 0.0 copy-done.1
  182.6 0.8 copy.18
  183.4 0.0 copy-done
  183.4 0.8 copy.19
  184.2 0.0 copy-done.2
  184.2 0.6 copy.20
Async XLA Ops:
  177.9 4.7 %copy-start.1 = (bf16[256,1024]{1,0:T(8,128)(2,1)S(1)}, bf16[256,1024]{1,0:T(8,128)(2,1)}, u32[]{:S(2)}) copy-start(bf16[256,1024]{1,0:T(8,128)(2,1)} %get-tuple-element.11) | copy-start | bytes 1572868
  177.9 5.5 %copy-start = (bf16[256,1024]{1,0:T(8,128)(2,1)S(1)}, bf16[256,1024]{1,0:T(8,128)(2,1)}, u32[]{:S(2)}) copy-start(bf16[256,1024]{1,0:T(8,128)(2,1)} %get-tuple-element.12) | copy-start | bytes 1572868
  177.9 6.3 %copy-start.2 = (bf16[256,128]{1,0:T(8,128)(2,1)S(1)}, bf16[256,128]{1,0:T(8,128)(2,1)}, u32[]{:S(2)}) copy-start(bf16[256,128]{1,0:T(8,128)(2,1)} %get-tuple-element.13) | copy-start | bytes 196612

commit v3 on v2

--- a/solution.py
+++ b/solution.py
@@ -15,7 +15,8 @@
 PER_GROUP = 16
 PAIRS = 8
 GW = PER_GROUP * HEADDIM
-MSG = 4 * 128 + 16
+REV = 2 * 128 + 16
+MSG = REV + 2 * 128
 
 BF = jnp.bfloat16
 FL = jnp.float32
@@ -86,25 +87,6 @@
     return v, step, rate, decay, within
 
 
-def phase_one(g, heads, x_ref, dy_ref, w_ref, r_ref, cat_te, cat_ew, last3, sd_ref):
-    lanes = pl.ds(pl.multiple_of(g * GW, GW), GW)
-    glanes = pl.ds(pl.multiple_of(g * NSTATE, NSTATE), NSTATE)
-    sel2 = spread(g, heads, 2)
-    xt = (x_ref[:, lanes].astype(FL) * dot(cat_te, sel2)).astype(BF)
-    dyw = (dy_ref[:, lanes].astype(FL) * dot(cat_ew, sel2)).astype(BF)
-    state = dot_tn(w_ref[:, glanes], xt).astype(BF)
-    dcar = dot_tn(r_ref[:, glanes], dyw).astype(BF)
-    lx = dot(last3, sel2[:heads]).astype(BF)
-    for p in range(PAIRS):
-        o, slot = g * (PAIRS // 2) + p // 2, p % 2
-        sl = slice(p * 128, p * 128 + 128)
-        sd_ref[o, slot * 128 : slot * 128 + 128, :] = state[:, sl]
-        sd_ref[o, 256 + slot * 128 : 384 + slot * 128, :] = dcar[:, sl]
-    for q in range(PAIRS // 2):
-        both = jnp.concatenate([lx[:, q * 256 : q * 256 + 128], lx[:, q * 256 + 128 : q * 256 + 256]], axis=0)
-        sd_ref[g * (PAIRS // 2) + q, 512:528, :] = both
-
-
 def decay_factors(step, within):
     last = within[BLOCK - 1 : BLOCK]
     mid = within[HALF - 1 : HALF]
@@ -120,9 +102,34 @@
     return jnp.concatenate([h, m, l, jnp.zeros((5, last.shape[1]), BF)], axis=0)
 
 
+def half_states(g, which, rows_ref, cat, proj_ref, sel2, sd_ref):
+    lanes = pl.ds(pl.multiple_of(g * GW, GW), GW)
+    glanes = pl.ds(pl.multiple_of(g * NSTATE, NSTATE), NSTATE)
+    scaled = (rows_ref[:, lanes].astype(FL) * dot(cat, sel2)).astype(BF)
+    state = dot_tn(proj_ref[:, glanes], scaled).astype(BF)
+    base = which * REV
+    for p in range(PAIRS):
+        at = base + (p % 2) * 128
+        sd_ref[g * (PAIRS // 2) + p // 2, at : at + 128, :] = state[:, p * 128 : p * 128 + 128]
+
+
 def source_decay(m, d, slot):
-    rows = m[d, 512 + 8 * slot : 520 + 8 * slot, :].astype(FL)
+    rows = m[d, 256 + 8 * slot : 264 + 8 * slot, :].astype(FL)
     return jnp.exp(rows[0:1] + rows[1:2] + rows[2:3])
+
+
+def flip(a, b):
+    return a + b - 2 * a * b
+
+
+def flip4(a, b):
+    return 2 * flip(a // 2, b // 2) + flip(a % 2, b % 2)
+
+
+def far_first(n):
+    def hops(k):
+        return k // 16 + (0, 1, 2, 1)[k // 4 % 4] + (0, 1, 2, 1)[k % 4]
+    return sorted(range(1, n), key=lambda k: -hops(k))
 
 
 def intra(g, heads, x_ref, dy_ref, w_ref, r_ref, within, wt_s, st_s, cat_tm, cat_fm, dxa, pr, pc, sel2):
@@ -187,7 +194,7 @@
     heads, groups, n, dps, factor,
     x_hbm, dy_hbm, w_hbm, r_hbm, raw_ref, bias_ref, dlog_ref, gain_ref,
     dx_hbm, dw_ref, dr_ref, dstep_ref, hg_ref,
-    x_ref, dy_ref, w_ref, r_ref, prm_s, within_s, wt_s, st_s, te_s, ew_s, tm_s, fm_s, l3_s, full_s,
+    x_ref, dy_ref, w_ref, r_ref, prm_s, sel_s, step_s, decay_s, sig_s, within_s, wt_s, st_s, te_s, ew_s, tm_s, fm_s, l3_s, full_s,
     r_acc, c_acc, dl_acc, sk_acc, dxa, pr, pc, dri, dwi, dxo,
     pg, sd, got, back, cg, cf, hb, hd,
     in_sem, out_sem, pg_s, pg_r, s1, r1, s2, r2, hb_s, hb_r, hd_s, hd_r,
@@ -195,7 +202,6 @@
     c = lax.axis_index("seq")
     d = lax.axis_index("dp")
     per = PAIRS // 2
-    home = c // per
     loads = [
         pltpu.make_async_copy(a, b, in_sem.at[i])
         for i, (a, b) in enumerate(((x_hbm, x_ref), (dy_hbm, dy_ref), (w_hbm, w_ref), (r_hbm, r_ref)))
@@ -203,15 +209,21 @@
     for load in loads:
         load.start()
 
+    zi, xi, yi = c // 16, c // 4 % 4, c % 4
+
+    def peer(k):
+        return flip(zi, k // 16) * 16 + flip4(xi, k // 4 % 4) * 4 + flip4(yi, k % 4)
+
+    order = far_first(n)
     barrier = pltpu.get_barrier_semaphore()
-
-    def greet(i, _):
-        pl.semaphore_signal(barrier, inc=1, device_id={"seq": lax.rem(c + i, n)}, device_id_type=MESH)
-        return 0
-
-    lax.fori_loop(1, n, greet, 0)
+    for k in order:
+        pl.semaphore_signal(barrier, inc=1, device_id={"seq": peer(k)}, device_id_type=MESH)
     for i in range(1, dps):
         pl.semaphore_signal(barrier, inc=1, device_id={"dp": lax.rem(d + i, dps)}, device_id_type=MESH)
+    for g in range(groups):
+        sel_s[g] = spread(g, heads, 2)
+    for acc in (r_acc, c_acc, dl_acc, sk_acc):
+        acc[...] = jnp.zeros_like(acc)
     pl.semaphore_wait(barrier, n - 1 + dps - 1)
 
     lane = lax.broadcasted_iota(jnp.int32, (8, heads), 1)
@@ -236,23 +248,25 @@
                 device_id={"seq": t}, device_id_type=MESH,
             )
 
-        def step(i, _):
-            t = lax.rem(c + i, n)
-            if wait:
+        if not wait:
+            for k in order:
+                one(peer(k)).start()
+        else:
+            def step(i, _):
+                t = lax.rem(c + i, n)
                 one(t).wait_send()
                 other(t).wait_recv()
-            else:
-                one(t).start()
-            return 0
-
-        lax.fori_loop(1, n, step, 0)
+                return 0
+
+            lax.fori_loop(1, n, step, 0)
 
     to_all(pg, pg_s, pg_r, False)
-    for acc in (r_acc, c_acc, dl_acc, sk_acc):
-        acc[...] = jnp.zeros_like(acc)
     to_all(pg, pg_s, pg_r, True)
     prm_s[...] = jnp.sum(pg[...], axis=0)
-    _, step, _, _, within = rates(raw_ref[...], prm_s[...])
+    v, step, _, decay, within = rates(raw_ref[...], prm_s[...])
+    step_s[...] = step
+    decay_s[...] = decay
+    sig_s[...] = 1.0 / (1.0 + jnp.exp(-v))
     last, to_end, from_start, to_mid, from_mid = decay_factors(step, within)
     within_s[...] = within
     wt_s[...] = within.T
@@ -266,36 +280,62 @@
     for load in loads:
         load.wait()
 
-    def out(o):
+    def out(t, half, slot):
+        rows = pl.ds(half * REV, MSG - REV if half else REV)
         return pltpu.make_async_remote_copy(
-            src_ref=sd.at[o], dst_ref=got.at[c], send_sem=s1.at[o], recv_sem=r1.at[c],
-            device_id={"seq": o}, device_id_type=MESH,
-        )
-
-    def out_from(t):
-        return pltpu.make_async_remote_copy(
-            src_ref=sd.at[t], dst_ref=got.at[t], send_sem=s1.at[t], recv_sem=r1.at[t],
+            src_ref=sd.at[t, rows], dst_ref=got.at[slot, rows], send_sem=s1.at[half, t], recv_sem=r1.at[half, slot],
             device_id={"seq": t}, device_id_type=MESH,
         )
 
+    def ret(t, half, slot):
+        rows = pl.ds(half * 256, 256)
+        return pltpu.make_async_remote_copy(
+            src_ref=back.at[t, rows], dst_ref=cg.at[slot, rows], send_sem=s2.at[half, t], recv_sem=r2.at[half, slot],
+            device_id={"seq": t}, device_id_type=MESH,
+        )
+
+    def row_of(j):
+        return flip(zi, j // 4) * 4 + flip4(xi, j % 4)
+
+    def two_rows(i):
+        if groups < 8:
+            return row_of(2 * i), row_of(2 * i + 1)
+        return row_of(i), row_of(4 + (i + 2) % 4)
+
+    def send_rows(i, copy, half):
+        ga, gb = two_rows(i)
+        for ka, kb in ((1, 3), (2, 0), (3, 1), (0, 2)):
+            for g, k in ((ga, ka), (gb, kb)):
+                t = g * per + flip4(yi, k)
+
+                @pl.when(t != c)
+                def _():
+                    copy(t, half, c).start()
+
     def states(i, _):
-        g = lax.rem(home + i, groups)
-        phase_one(g, heads, x_ref, dy_ref, w_ref, r_ref, te_s[...], ew_s[...], l3_s[...], sd)
-        for q in range(per):
-            o = g * per + lax.rem(c + q, per)
-
-            @pl.when(o != c)
-            def _():
-                out(o).start()
-
-        return 0
-
-    lax.fori_loop(0, groups, states, 0)
+        for g in two_rows(i):
+            half_states(g, 0, x_ref, te_s[...], w_ref, sel_s[g], sd)
+            lx = dot(l3_s[...], sel_s[g, :heads]).astype(BF)
+            for q in range(per):
+                sd[g * per + q, 256:272, :] = jnp.concatenate(
+                    [lx[:, q * 256 : q * 256 + 128], lx[:, q * 256 + 128 : q * 256 + 256]], axis=0
+                )
+        send_rows(i, out, 0)
+        return 0
+
+    def grads(i, _):
+        for g in two_rows(i):
+            half_states(g, 1, dy_ref, ew_s[...], r_ref, sel_s[g], sd)
+        send_rows(i, out, 1)
+        return 0
+
+    lax.fori_loop(0, groups // 2, states, 0)
+    lax.fori_loop(0, groups // 2, grads, 0)
     got[c] = sd[c]
 
     def local(g, _):
         glanes = pl.ds(pl.multiple_of(g * NSTATE, NSTATE), NSTATE)
-        sel2 = spread(g, heads, 2)
+        sel2 = sel_s[g]
         dr_i, dw_i = intra(
             g, heads, x_ref, dy_ref, w_ref, r_ref, within_s[...], wt_s, st_s, tm_s[...], fm_s[...], dxa, pr, pc, sel2
         )
@@ -307,104 +347,96 @@
 
     lax.fori_loop(0, groups, local, 0)
 
-    def arrived(i, _):
-        out_from(lax.rem(c + i, n)).wait_recv()
-        return 0
-
-    lax.fori_loop(1, n, arrived, 0)
-
-    def ret(t, half):
-        rows = pl.ds(half * 256, 256)
-        return pltpu.make_async_remote_copy(
-            src_ref=back.at[t, rows], dst_ref=cg.at[c, rows], send_sem=s2.at[half, t], recv_sem=r2.at[half, c],
-            device_id={"seq": t}, device_id_type=MESH,
-        )
-
-    def ret_from(t, half):
-        rows = pl.ds(half * 256, 256)
-        return pltpu.make_async_remote_copy(
-            src_ref=back.at[t, rows], dst_ref=cg.at[t, rows], send_sem=s2.at[half, t], recv_sem=r2.at[half, t],
-            device_id={"seq": t}, device_id_type=MESH,
-        )
-
     for half in range(2):
+
+        def arrived(i, _):
+            t = lax.rem(c + i, n)
+            out(t, half, t).wait_recv()
+            return 0
+
+        lax.fori_loop(1, n, arrived, 0)
         cf[...] = jnp.zeros_like(cf)
 
         def scan(i, _):
             t = i if half == 0 else n - 1 - i
             for slot in range(2):
                 rows = slice(slot * 128, slot * 128 + 128)
-                mrows = slice(half * 256 + slot * 128, half * 256 + slot * 128 + 128)
-                back[t, mrows, :] = cf[rows, :].astype(BF)
-                cf[rows, :] = cf[rows, :] * source_decay(got, t, slot) + got[t, mrows, :].astype(FL)
+                src = slice(half * REV + slot * 128, half * REV + slot * 128 + 128)
+                dst = slice(half * 256 + slot * 128, half * 256 + slot * 128 + 128)
+                back[t, dst, :] = cf[rows, :].astype(BF)
+                cf[rows, :] = cf[rows, :] * source_decay(got, t, slot) + got[t, src, :].astype(FL)
             return 0
 
         lax.fori_loop(0, n, scan, 0)
 
         def give(i, _):
-            g = lax.rem(home + i // per, groups)
-            t = g * per + lax.rem(c + i, per)
+            send_rows(i, ret, half)
+            return 0
+
+        lax.fori_loop(0, groups // 2, give, 0)
+        cg[c, half * 256 : half * 256 + 256, :] = back[c, half * 256 : half * 256 + 256, :]
+
+    def lane_cat(ref, g, base):
+        return jnp.concatenate(
+            [ref[g * per + p // 2, base + (p % 2) * 128 : base + (p % 2) * 128 + 128, :] for p in range(PAIRS)], axis=1
+        )
+
+    def landed(g, half):
+        for q in range(per):
+            t = g * per + q
 
             @pl.when(t != c)
             def _():
-                ret(t, half).start()
-
-            return 0
-
-        lax.fori_loop(0, n, give, 0)
-        cg[c, half * 256 : half * 256 + 256, :] = back[c, half * 256 : half * 256 + 256, :]
+                ret(t, half, t).wait_recv()
+
+    def slices(g):
+        return pl.ds(pl.multiple_of(g * GW, GW), GW), pl.ds(pl.multiple_of(g * NSTATE, NSTATE), NSTATE)
 
     def carried(i, _):
-        g = lax.rem(home + groups - i, groups)
-        g4 = g * per
-        for q in range(per):
-            @pl.when(g4 + q != c)
-            def _():
-                ret_from(g4 + q, 0).wait_recv()
-                ret_from(g4 + q, 1).wait_recv()
-
-        lanes = pl.ds(pl.multiple_of(g * GW, GW), GW)
-        glanes = pl.ds(pl.multiple_of(g * NSTATE, NSTATE), NSTATE)
-        sel2 = spread(g, heads, 2)
-        sel = sel2[:heads]
-        xf, dyf = x_ref[:, lanes].astype(FL), dy_ref[:, lanes].astype(FL)
-        te = dot(te_s[...], sel2)
-        xt = (xf * te).astype(BF)
-        dyw = (dyf * dot(ew_s[...], sel2)).astype(BF)
-        wide = dot(full_s[...], sel2)
-
-        def lane_cat(ref, base):
-            return jnp.concatenate(
-                [ref[g4 + p // 2, base + (p % 2) * 128 : base + (p % 2) * 128 + 128, :] for p in range(PAIRS)], axis=1
-            )
-
-        car, gst, own = lane_cat(cg, 0), lane_cat(cg, 256), lane_cat(sd, 0)
-        zc = dot(r_ref[:, glanes], car)
-        zg = dot(w_ref[:, glanes], gst)
-        r_acc[...] += gather_heads(dyw.astype(FL) * zc, sel)
-        c_acc[...] += gather_heads(xt.astype(FL) * zg, sel)
-        ends = jnp.sum(gst.astype(FL) * (own.astype(FL) + wide[0:1] * car.astype(FL)), axis=0, keepdims=True)
-        skips = jnp.sum(xf * dyf, axis=0, keepdims=True)
-        both = jnp.concatenate([ends, skips, jnp.zeros((6, GW), FL)], axis=0)
-        both = gather_heads(both, sel)
-        dl_acc[...] += both[0:1]
-        sk_acc[...] += both[1:2]
-        dxo[:, lanes] = (dxa[:, lanes] + te * zg + wide[1:2] * dyf).astype(BF)
-        pltpu.make_async_copy(dxo.at[:, lanes], dx_hbm.at[:, lanes], out_sem.at[g]).start()
-        dr_ref[:, glanes] = (dri[:, glanes] + dot_nt(dyw, car)).astype(BF)
-        dw_ref[:, glanes] = (dwi[:, glanes] + dot_nt(xt, gst)).astype(BF)
-        return 0
-
-    lax.fori_loop(0, groups, carried, 0)
-    v, step, rate, decay, _ = rates(raw_ref[...], prm_s[...])
+        for g in two_rows(i):
+            landed(g, 0)
+            lanes, glanes = slices(g)
+            sel2 = sel_s[g]
+            dyw = (dy_ref[:, lanes].astype(FL) * dot(ew_s[...], sel2)).astype(BF)
+            car = lane_cat(cg, g, 0)
+            r_acc[...] += gather_heads(dyw.astype(FL) * dot(r_ref[:, glanes], car), sel2[:heads])
+            dr_ref[:, glanes] = (dri[:, glanes] + dot_nt(dyw, car)).astype(BF)
+        return 0
+
+    lax.fori_loop(0, groups // 2, carried, 0)
+
+    def returned(i, _):
+        for g in two_rows(i):
+            landed(g, 1)
+            lanes, glanes = slices(g)
+            sel2 = sel_s[g]
+            sel = sel2[:heads]
+            xf, dyf = x_ref[:, lanes].astype(FL), dy_ref[:, lanes].astype(FL)
+            te = dot(te_s[...], sel2)
+            xt = (xf * te).astype(BF)
+            wide = dot(full_s[...], sel2)
+            car, gst, own = lane_cat(cg, g, 0), lane_cat(cg, g, 256), lane_cat(sd, g, 0)
+            zg = dot(w_ref[:, glanes], gst)
+            dxo[:, lanes] = (dxa[:, lanes] + te * zg + wide[1:2] * dyf).astype(BF)
+            pltpu.make_async_copy(dxo.at[:, lanes], dx_hbm.at[:, lanes], out_sem.at[g]).start()
+            c_acc[...] += gather_heads(xt.astype(FL) * zg, sel)
+            ends = jnp.sum(gst.astype(FL) * (own.astype(FL) + wide[0:1] * car.astype(FL)), axis=0, keepdims=True)
+            skips = jnp.sum(xf * dyf, axis=0, keepdims=True)
+            both = gather_heads(jnp.concatenate([ends, skips, jnp.zeros((6, GW), FL)], axis=0), sel)
+            dl_acc[...] += both[0:1]
+            sk_acc[...] += both[1:2]
+            dw_ref[:, glanes] = (dwi[:, glanes] + dot_nt(xt, gst)).astype(BF)
+        return 0
+
+    lax.fori_loop(0, groups // 2, returned, 0)
+    rate = -jnp.exp(prm_s[1:2])
     trow = lax.broadcasted_iota(jnp.int32, (BLOCK, heads), 0)
     dwithin = r_acc[...] - c_acc[...] + jnp.where(trow == BLOCK - 1, dl_acc[...], 0.0)
     dld = tri_sum(triangle(True), dwithin)
-    dstep = c_acc[...] / step + rate * dld
-    draw = dstep / (1.0 + jnp.exp(-v))
+    draw = (c_acc[...] / step_s[...] + rate * dld) * sig_s[...]
     hb[c] = jnp.concatenate(
         [
-            jnp.sum(dld * decay, axis=0, keepdims=True),
+            jnp.sum(dld * decay_s[...], axis=0, keepdims=True),
             jnp.sum(draw, axis=0, keepdims=True),
             sk_acc[...],
             jnp.zeros((5, heads), FL),
@@ -428,9 +460,9 @@
     def leave(t, _):
         @pl.when(t != c)
         def _():
-            out(t).wait_send()
-            ret(t, 0).wait_send()
-            ret(t, 1).wait_send()
+            for half in range(2):
+                out(t, half, c).wait_send()
+                ret(t, half, c).wait_send()
 
         return 0
 
@@ -480,14 +512,15 @@
         out_specs=[hbm] + [vm] * 4,
         scratch_shapes=[
             pltpu.VMEM(x.shape, BF), pltpu.VMEM(x.shape, BF), pltpu.VMEM(w.shape, BF), pltpu.VMEM(r.shape, BF),
-            pltpu.VMEM((8, heads), FL), full, tr, tr, cat2, cat2, cat1, cat1,
+            pltpu.VMEM((8, heads), FL), pltpu.VMEM((groups, 2 * heads, GW), BF), full, full, full,
+            full, tr, tr, cat2, cat2, cat1, cat1,
             pltpu.VMEM((8, heads), BF), pltpu.VMEM((8, 2 * heads), BF),
             full, full, row, row,
             pltpu.VMEM(x.shape, FL), wide, wide, pltpu.VMEM(r.shape, FL), pltpu.VMEM(w.shape, FL), pltpu.VMEM(x.shape, BF),
             small, pltpu.VMEM((n, MSG, 128), BF), pltpu.VMEM((n, MSG, 128), BF),
             pltpu.VMEM((n, 512, 128), BF), pltpu.VMEM((n, 512, 128), BF), pltpu.VMEM((256, 128), FL),
             small, pltpu.VMEM((dps, 8, heads), FL),
-            sem((4,)), sem((groups,)), sem((n,)), sem((n,)), sem((n,)), sem((n,)), sem((2, n)), sem((2, n)),
+            sem((4,)), sem((groups,)), sem((n,)), sem((n,)), sem((2, n)), sem((2, n)), sem((2, n)), sem((2, n)),
             sem((n,)), sem((n,)), sem((dps,)), sem((dps,)),
         ],
         compiler_params=pltpu.CompilerParams(

time: 185 us -> 150 us (0.81)
  Pallas kernels: 176 us -> 141 us
    pallas_call x1, Pallas kernels: 176 us -> 141 us  [body(): pl.pallas_call(functools.partial(kernel, heads, groups, n, dps, factor),...]
where the time goes in v3:
time: 150 us
  Pallas kernels  141 us (94%)
  local copies, waits for them, and re-layouts  8.21 us (5%)
    pallas_call x1, Pallas kernels, body(): pl.pallas_call(functools.partial(kernel, heads, groups, n, dps, factor),...  141 us
    unnamed x10, local copies, waits for them, and re-layouts  6.96 us

profile of v3, /device:TPU:1, one launch (start us, length us, event | category | flops | bytes accessed | tf_op | source)
XLA Modules:
  0.0 149.6 jit_solution(10667997173338905524)
XLA Ops:
  0.6 140.8 %mixer_backward.1 = (bf16[256,8192]{1,0:T(8,128)(2,1)}, bf16[256,1024]{1,0:T(8,128)(2,1)}, bf16[256,1024]{1,0:T(8,128)(2,1)}, bf16[256,128]{1,0:T(8,128)(2,1)}, f32[8,128]{1,0:T(8,128)}) custom-call(bf16[256,8192]{1,0:T(8,128)(2,1)} %bitcast.9, bf16[256,8192]{1,0:T(8,128)(2,1)} %bitcast.10, bf16[256,1024]{1,0:T(8,128)(2,1)} %bitcast.12, ...), custom_call_target="tpu_custom_call" | custom-call | tf_op jit(solution)/shard_map/mixer_backward/pallas_call | solution.py:502
  141.4 1.2 slice.3
  142.7 0.0 copy-start.1
  142.7 0.0 copy-start
  142.7 0.0 copy-start.2
  142.7 4.7 %copy.17 = bf16[1,256,8192]{2,1,0:T(8,128)(2,1)} copy(bf16[1,256,8192]{2,1,0:T(8,128)(2,1)} %bitcast.11) | data formatting | bytes 8388608
  147.4 0.0 copy-done.1
  147.4 0.8 copy.18
  148.2 0.0 copy-done
  148.2 0.8 copy.19
  149.0 0.0 copy-done.2
  149.0 0.6 copy.20
Async XLA Ops:
  142.7 4.7 %copy-start.1 = (bf16[256,1024]{1,0:T(8,128)(2,1)S(1)}, bf16[256,1024]{1,0:T(8,128)(2,1)}, u32[]{:S(2)}) copy-start(bf16[256,1024]{1,0:T(8,128)(2,1)} %get-tuple-element.11) | copy-start | bytes 1572868
  142.7 5.5 %copy-start = (bf16[256,1024]{1,0:T(8,128)(2,1)S(1)}, bf16[256,1024]{1,0:T(8,128)(2,1)}, u32[]{:S(2)}) copy-start(bf16[256,1024]{1,0:T(8,128)(2,1)} %get-tuple-element.12) | copy-start | bytes 1572868
  142.7 6.3 %copy-start.2 = (bf16[256,128]{1,0:T(8,128)(2,1)S(1)}, bf16[256,128]{1,0:T(8,128)(2,1)}, u32[]{:S(2)}) copy-start(bf16[256,128]{1,0:T(8,128)(2,1)} %get-tuple-element.13) | copy-start | bytes 196612

commit v4 on v3

v4 whole, which is shorter than its diff:
```python
import functools
import math

import jax
import jax.numpy as jnp
from jax import lax
from jax.experimental import pallas as pl
from jax.experimental.pallas import tpu as pltpu
from jax.sharding import PartitionSpec as P

HEADDIM = 64
NSTATE = 128
BLOCK = 256
HALF = 128
PER_GROUP = 16
PAIRS = 8
GW = PER_GROUP * HEADDIM
ROW = 4
DEC = 16
PARTS = 8

BF = jnp.bfloat16
FL = jnp.float32
MESH = pl.DeviceIdType.MESH


def dot(a, b):
    return jnp.dot(a, b, preferred_element_type=FL)


def dot_nt(a, b):
    return lax.dot_general(a, b, (((1,), (1,)), ((), ())), preferred_element_type=FL)


def dot_tn(a, b):
    return lax.dot_general(a, b, (((0,), (0,)), ((), ())), preferred_element_type=FL)


def hi_lo(a):
    hi = a.astype(BF)
    return hi, (a - hi.astype(FL)).astype(BF)


def three(a):
    hi, _ = hi_lo(a)
    rest = a - hi.astype(FL)
    mid, low = hi_lo(rest)
    return hi, mid, low


def cat_hi_lo(a):
    return jnp.concatenate(hi_lo(a), axis=1)


def tri_sum(tri, a):
    hi, mid, low = three(a)
    return dot(tri, hi) + dot(tri, mid) + dot(tri, low)


def triangle(upper):
    row = lax.broadcasted_iota(jnp.int32, (BLOCK, BLOCK), 0)
    col = lax.broadcasted_iota(jnp.int32, (BLOCK, BLOCK), 1)
    keep = (col >= row) if upper else (col <= row)
    return jnp.where(keep, 1.0, 0.0).astype(BF)


def spread(g, heads, copies):
    row = lax.broadcasted_iota(jnp.int32, (copies * heads, GW), 0)
    col = lax.broadcasted_iota(jnp.int32, (copies * heads, GW), 1)
    if copies == 2:
        row = jnp.where(row >= heads, row - heads, row)
    return jnp.where(row == g * PER_GROUP + col // HEADDIM, 1.0, 0.0).astype(BF)


def gather_heads(p, sel):
    hi, lo = hi_lo(p)
    return dot_nt(hi, sel) + dot_nt(lo, sel)


def rates(raw, prm):
    v = raw.astype(FL) + prm[0:1]
    e = jnp.exp(-jnp.abs(v))
    small = e * (1.0 - e * (0.5 - e * (1.0 / 3 - e * (0.25 - e * 0.2))))
    step = jnp.maximum(v, 0.0) + jnp.where(e < 0.03125, small, jnp.log(1.0 + e))
    rate = -jnp.exp(prm[1:2])
    decay = rate * step
    within = tri_sum(triangle(False), decay)
    return v, step, rate, decay, within


def decay_factors(step, within):
    last = within[BLOCK - 1 : BLOCK]
    mid = within[HALF - 1 : HALF]
    to_end = jnp.exp(last - within) * step
    from_start = jnp.exp(within)
    to_mid = jnp.exp(mid - within[:HALF]) * step[:HALF]
    from_mid = jnp.exp(within[HALF:] - mid)
    return last, to_end, from_start, to_mid, from_mid


def last_terms(last):
    h, m, l = three(last)
    return jnp.concatenate([h, m, l, jnp.zeros((DEC - 3, last.shape[1]), BF)], axis=0)


def half_states(g, rows_ref, cat, proj_ref, sel2, out_ref, at, keep):
    lanes = pl.ds(pl.multiple_of(g * GW, GW), GW)
    glanes = pl.ds(pl.multiple_of(g * NSTATE, NSTATE), NSTATE)
    scaled = (rows_ref[:, lanes].astype(FL) * dot(cat, sel2)).astype(BF)
    if keep is not None:
        keep[:, lanes] = scaled
    state = dot_tn(proj_ref[:, glanes], scaled).astype(BF)
    for p in range(PAIRS):
        out_ref[at + (pl.ds(p * 128, 128),)] = state[:, p * 128 : p * 128 + 128]


def intra(g, heads, x_ref, dy_ref, w_ref, r_ref, within, wt_s, st_s, cat_tm, cat_fm, dxa, pr, pc, sel2):
    lanes = pl.ds(pl.multiple_of(g * GW, GW), GW)
    glanes = pl.ds(pl.multiple_of(g * NSTATE, NSTATE), NSTATE)
    wg, rg = w_ref[:, glanes], r_ref[:, glanes]
    row = lax.broadcasted_iota(jnp.int32, (HALF, HALF), 0)
    col = lax.broadcasted_iota(jnp.int32, (HALF, HALF), 1)
    lower = col <= row
    first = lax.broadcasted_iota(jnp.int32, (HALF, 128), 1) < HEADDIM
    scores = dot_nt(rg, wg)
    tm = dot(cat_tm, sel2)
    x0 = x_ref[:HALF, lanes].astype(FL)
    xt1 = (x0 * tm).astype(BF)
    dy1 = (dy_ref[HALF:, lanes].astype(FL) * dot(cat_fm, sel2)).astype(BF)
    sb = scores[HALF:, :HALF].astype(BF)
    z = dot(sb, xt1)
    yb = dot_tn(sb, dy1)
    ds_low = dot_nt(dy1, xt1)
    pr[:HALF, :] = jnp.zeros((HALF, GW), FL)
    pr[HALF:, :] = dy1.astype(FL) * z
    pc[:HALF, :] = xt1.astype(FL) * yb
    pc[HALF:, :] = jnp.zeros((HALF, GW), FL)
    dxa[:HALF, lanes] = tm * yb
    dxa[HALF:, lanes] = jnp.zeros((HALF, GW), FL)
    wr = pltpu.roll(within, lax.rem(heads - g * PER_GROUP, heads), 1)
    wt = wt_s[pl.ds(pl.multiple_of(g * PER_GROUP, PER_GROUP), PER_GROUP), :]
    st = st_s[pl.ds(pl.multiple_of(g * PER_GROUP, PER_GROUP), PER_GROUP), :]
    ds_diag = []
    for sub in range(2):
        rs = slice(sub * HALF, sub * HALF + HALF)
        sd = jnp.where(lower, scores[rs, rs], 0.0)
        ds = jnp.zeros((HALF, HALF), FL)
        for p in range(PAIRS):
            pls = pl.ds(pl.multiple_of(g * GW + p * 128, 128), 128)
            here = slice(p * 128, p * 128 + 128)
            xp, dyp = x_ref[rs, pls], dy_ref[rs, pls]
            none = jnp.zeros_like(xp)
            xst = jnp.concatenate([jnp.where(first, xp, none), jnp.where(first, none, xp)], axis=0)
            dyst = jnp.concatenate([jnp.where(first, dyp, none), jnp.where(first, none, dyp)], axis=0)
            dw = dot_nt(dyp, xst)
            parts = []
            for k in range(2):
                h = 2 * p + k
                gap = jnp.minimum(wr[rs, h : h + 1] - wt[h : h + 1, rs], 0.0)
                es = jnp.exp(gap) * st[h : h + 1, rs]
                ds += dw[:, k * HALF : k * HALF + HALF] * es
                parts.append((sd * es).astype(BF))
            y = dot(jnp.concatenate(parts, axis=1), xst)
            dxp = dot_tn(jnp.concatenate(parts, axis=0), dyst)
            pr[rs, here] += dyp.astype(FL) * y
            pc[rs, here] += xp.astype(FL) * dxp
            dxa[rs, pls] += dxp
        ds_diag.append(jnp.where(lower, ds, 0.0))
    top = jnp.concatenate([ds_diag[0], jnp.zeros((HALF, HALF), FL)], axis=1)
    low = jnp.concatenate([ds_low, ds_diag[1]], axis=1)
    dscore = jnp.concatenate([top, low], axis=0).astype(BF)
    return dot(dscore, wg), dot_tn(dscore, rg)


def kernel(
    heads, groups, n, dps, factor,
    x_hbm, dy_hbm, w_hbm, r_hbm, raw_ref, bias_ref, dlog_ref, gain_ref,
    dx_hbm, dw_ref, dr_ref, dstep_ref, hg_ref,
    x_ref, dy_ref, w_ref, r_ref, prm_s, sel_s, step_s, decay_s, sig_s, within_s, wt_s, st_s, te_s, ew_s, tm_s, fm_s, l3_s, full_s,
    r_acc, c_acc, dl_acc, sk_acc, dxa, pr, pc, dri, dwi, xt_s,
    sd, got, back, cg, es, tb, tgot, cb, crow, py, pr_all, hy, hr, hd,
    in_sem, out_sem, s1, r1, s2, r2, s3, r3, s4, r4, py_s, py_r, pz_s, pz_r, hy_s, hy_r, hr_s, hr_r, hd_s, hd_r,
):
    c = lax.axis_index("seq")
    d = lax.axis_index("dp")
    loads = [
        pltpu.make_async_copy(a, b, in_sem.at[i])
        for i, (a, b) in enumerate(((x_hbm, x_ref), (dy_hbm, dy_ref), (w_hbm, w_ref), (r_hbm, r_ref)))
    ]
    for load in loads:
        load.start()

    y, row, rows = c % ROW, c // ROW, n // ROW
    gq = groups // ROW
    pq = gq * PAIRS
    po = pq // rows

    def in_row(t):
        return {"seq": row * ROW + t}

    def in_column(t):
        return {"seq": t * ROW + y}

    def across(t):
        return {"dp": t}

    barrier = pltpu.get_barrier_semaphore()
    for i in range(1, rows):
        pl.semaphore_signal(barrier, inc=1, device_id=in_column((row + i) % rows), device_id_type=MESH)
    for i in range(1, dps):
        pl.semaphore_signal(barrier, inc=1, device_id=across((d + i) % dps), device_id_type=MESH)
    for i in range(1, ROW):
        pl.semaphore_signal(barrier, inc=1, device_id=in_row((y + i) % ROW), device_id_type=MESH)
    for g in range(groups):
        sel_s[g] = spread(g, heads, 2)
    for acc in (r_acc, c_acc, dl_acc, sk_acc):
        acc[...] = jnp.zeros_like(acc)
    pl.semaphore_wait(barrier, rows - 1 + dps - 1 + ROW - 1)

    lane = lax.broadcasted_iota(jnp.int32, (8, heads), 1)
    which = lax.broadcasted_iota(jnp.int32, (8, heads), 0)
    mine = jnp.zeros((8, heads), FL)
    owned = heads // n
    for i, ref in enumerate((bias_ref, dlog_ref, gain_ref)):
        for k in range(owned):
            mine = jnp.where((which == i) & (lane == c * owned + k), ref[k], mine)

    def total(value, buf, me, count, where, send, recv):
        buf[me] = value

        def copy(i, slot):
            return pltpu.make_async_remote_copy(
                src_ref=buf.at[slot], dst_ref=buf.at[slot], send_sem=send.at[i], recv_sem=recv.at[slot],
                device_id=where((me + i) % count), device_id_type=MESH,
            )

        for i in range(1, count):
            copy(i, me).start()
        for i in range(1, count):
            copy(i, me).wait_send()
            copy(i, (me + i) % count).wait_recv()
        return jnp.sum(buf[...], axis=0)

    mine = total(mine, py, y, ROW, in_row, py_s, py_r)
    prm_s[...] = total(mine, pr_all, row, rows, in_column, pz_s, pz_r)
    v, step, _, decay, within = rates(raw_ref[...], prm_s[...])
    step_s[...] = step
    decay_s[...] = decay
    sig_s[...] = 1.0 / (1.0 + jnp.exp(-v))
    last, to_end, from_start, to_mid, from_mid = decay_factors(step, within)
    within_s[...] = within
    wt_s[...] = within.T
    st_s[...] = step.T
    te_s[...] = cat_hi_lo(to_end)
    ew_s[...] = cat_hi_lo(from_start)
    tm_s[...] = cat_hi_lo(to_mid)
    fm_s[...] = cat_hi_lo(from_mid)
    l3_s[...] = last_terms(last)
    full_s[...] = cat_hi_lo(jnp.concatenate([jnp.exp(last), prm_s[2:3], jnp.zeros((6, heads), FL)], axis=0))
    for load in loads:
        load.wait()

    def span(half, k):
        return pl.ds(k * PAIRS * 128, PAIRS * 128 + (pq * DEC if half == 0 and k == gq - 1 else 0))

    def out(half, k, t, slot):
        at = span(half, k)
        return pltpu.make_async_remote_copy(
            src_ref=sd.at[half, t, at], dst_ref=got.at[half, slot, at],
            send_sem=s1.at[half, k, t], recv_sem=r1.at[half, k, slot], device_id=in_row(t), device_id_type=MESH,
        )

    def make(half, t, k):
        g = t * gq + k
        at = (half, t)
        src = (x_ref, te_s, w_ref) if half == 0 else (dy_ref, ew_s, r_ref)
        half_states(g, src[0], src[1][...], src[2], sel_s[g], sd.at[half, t, pl.ds(k * PAIRS * 128, PAIRS * 128)], (), xt_s if half == 0 else None)
        if half == 0:
            lx = dot(l3_s[...], sel_s[g, :heads]).astype(BF)
            for p in range(PAIRS):
                at = pq * 128 + (k * PAIRS + p) * DEC
                sd[0, t, at : at + DEC, :] = lx[:, p * 128 : p * 128 + 128]

    for half in range(2):
        for k in range(gq):

            def send(i, _):
                t = (y + i) % ROW
                make(half, t, k)
                out(half, k, t, y).start()
                return 0

            lax.fori_loop(1, ROW, send, 0)
        for k in range(gq):
            make(half, y, k)
        got[half, y] = sd[half, y]

    def local(g, _):
        glanes = pl.ds(pl.multiple_of(g * NSTATE, NSTATE), NSTATE)
        sel2 = sel_s[g]
        dr_i, dw_i = intra(
            g, heads, x_ref, dy_ref, w_ref, r_ref, within_s[...], wt_s, st_s, tm_s[...], fm_s[...], dxa, pr, pc, sel2
        )
        lanes = pl.ds(pl.multiple_of(g * GW, GW), GW)
        dyf = dy_ref[:, lanes].astype(FL)
        dxa[:, lanes] += dot(full_s[...], sel2)[1:2] * dyf
        skips = jnp.sum(x_ref[:, lanes].astype(FL) * dyf, axis=0, keepdims=True)
        sk_acc[...] += gather_heads(jnp.broadcast_to(skips, (8, GW)), sel2[:heads])[0:1]
        dri[:, glanes] = dr_i
        dwi[:, glanes] = dw_i
        r_acc[...] += gather_heads(pr[...], sel2[:heads])
        c_acc[...] += gather_heads(pc[...], sel2[:heads])
        return 0

    share = (groups * 5 // 8, groups * 6 // 8, groups * 7 // 8, groups)
    lax.fori_loop(0, share[0], local, 0)

    def arrived(half):
        for k in range(gq):
            for i in range(1, ROW):
                t = (y + i) % ROW
                out(half, k, t, t).wait_recv()

    def whole(p):
        return pl.ds(pl.multiple_of(p * 128, 128), 128)

    def up(half, src, t, slot):
        at = pl.ds(0, po * 128 + (po * DEC if half == 0 else 0))
        return pltpu.make_async_remote_copy(
            src_ref=src.at[half, t, at], dst_ref=tgot.at[half, slot, at],
            send_sem=s3.at[half, t], recv_sem=r3.at[half, slot], device_id=in_column(t), device_id_type=MESH,
        )

    def down(half, t, slot):
        return pltpu.make_async_remote_copy(
            src_ref=cb.at[half, t], dst_ref=crow.at[half, slot],
            send_sem=s4.at[half, t], recv_sem=r4.at[half, slot], device_id=in_column(t), device_id_type=MESH,
        )

    def ret(half, k, t, slot):
        at = pl.ds(pl.multiple_of(k * (PAIRS * 128), PAIRS * 128), PAIRS * 128)
        return pltpu.make_async_remote_copy(
            src_ref=back.at[half, t, at], dst_ref=cg.at[half, slot, at],
            send_sem=s2.at[half, k, t], recv_sem=r2.at[half, k, slot], device_id=in_row(t), device_id_type=MESH,
        )

    def blocks(half):
        return range(ROW) if half == 0 else range(ROW - 1, -1, -1)

    def log_decay(rows3):
        f = rows3.astype(FL)
        return f[0:1] + f[1:2] + f[2:3]

    def row_totals(half):
        arrived(half)

        def one(p, _):
            if half == 0:
                logs = jnp.zeros((1, 128), FL)
                for b in range(ROW):
                    log = log_decay(got[0, b, pl.ds(pl.multiple_of(pq * 128 + p * DEC, DEC), DEC), :])
                    es[b, p] = jnp.broadcast_to(jnp.exp(log), (8, 128))
                    logs += log
                h, m, l = three(logs)
                terms = jnp.concatenate([h, m, l, jnp.zeros((DEC - 3, 128), BF)], axis=0)
                tb[0, p // po, pl.ds(pl.multiple_of(po * 128 + (p % po) * DEC, DEC), DEC), :] = terms
            acc = jnp.zeros((128, 128), FL)
            for b in blocks(half):
                acc = acc * es[b, p, 0:1] + got[half, b, whole(p), :].astype(FL)
            tb[half, p // po, whole(p % po), :] = acc.astype(BF)
            return 0

        lax.fori_loop(0, pq, one, 0)
        for i in range(1, rows):
            up(half, tb, (row + i) % rows, row).start()
        tgot[half, row] = tb[half, row]

    def scan_rows(half):
        for i in range(1, rows):
            t = (row + i) % rows
            up(half, tb, t, t).wait_recv()
        for p in range(po):
            at = slice(p * 128, p * 128 + 128)

            def one(i, acc):
                t = i if half == 0 else rows - 1 - i
                cb[half, t, at, :] = acc.astype(BF)
                e = jnp.exp(log_decay(tgot[0, t, po * 128 + p * DEC : po * 128 + (p + 1) * DEC, :]))
                return acc * e + tgot[half, t, at, :].astype(FL)

            lax.fori_loop(0, rows, one, jnp.zeros((128, 128), FL))
        for i in range(1, rows):
            down(half, (row + i) % rows, row).start()
        crow[half, row] = cb[half, row]

    def scan_blocks(half):
        for i in range(1, rows):
            t = (row + i) % rows
            down(half, t, t).wait_recv()
        for k in range(gq):

            def one(i, _):
                p = k * PAIRS + i
                acc = crow[half, p // po, whole(p % po), :].astype(FL)
                for b in blocks(half):
                    back[half, b, whole(p), :] = acc.astype(BF)
                    acc = acc * es[b, p, 0:1] + got[half, b, whole(p), :].astype(FL)
                return 0

            lax.fori_loop(0, PAIRS, one, 0)
            for i in range(1, ROW):
                ret(half, k, (y + i) % ROW, y).start()
        cg[half, y] = back[half, y]

    row_totals(0)
    lax.fori_loop(share[0], share[1], local, 0)
    scan_rows(0)
    lax.fori_loop(share[1], share[2], local, 0)
    scan_blocks(0)
    row_totals(1)
    lax.fori_loop(share[2], share[3], local, 0)
    scan_rows(1)
    scan_blocks(1)

    def lane_cat(ref, half, t, k):
        return jnp.concatenate(
            [ref[half, t, pl.ds(pl.multiple_of((k * PAIRS + p) * 128, 128), 128), :] for p in range(PAIRS)], axis=1
        )

    def landed(half, k, t):
        @pl.when(t != y)
        def _():
            ret(half, k, t, t).wait_recv()

    def slices(g):
        return pl.ds(pl.multiple_of(g * GW, GW), GW), pl.ds(pl.multiple_of(g * NSTATE, NSTATE), NSTATE)

    def carried(j, _):
        k, t = j // ROW, (y + j) % ROW
        g = t * gq + k
        landed(0, k, t)
        lanes, glanes = slices(g)
        sel2 = sel_s[g]
        dyw = (dy_ref[:, lanes].astype(FL) * dot(ew_s[...], sel2)).astype(BF)
        car = lane_cat(cg, 0, t, k)
        r_acc[...] += gather_heads(dyw.astype(FL) * dot(r_ref[:, glanes], car), sel2[:heads])
        dr_ref[:, glanes] = (dri[:, glanes] + dot_nt(dyw, car)).astype(BF)
        return 0

    lax.fori_loop(0, groups, carried, 0)

    def returned(j, _):
        k, t = j // ROW, (y + j) % ROW
        g = t * gq + k
        landed(1, k, t)
        lanes, glanes = slices(g)
        sel2 = sel_s[g]
        sel = sel2[:heads]
        te = dot(te_s[...], sel2)
        xt = xt_s[:, lanes]
        ea = dot(full_s[...], sel2)[0:1]
        car, gst, own = lane_cat(cg, 0, t, k), lane_cat(cg, 1, t, k), lane_cat(sd, 0, t, k)
        zg = dot(w_ref[:, glanes], gst)
        c_acc[...] += gather_heads(xt.astype(FL) * zg, sel)
        ends = jnp.sum(gst.astype(FL) * (own.astype(FL) + ea * car.astype(FL)), axis=0, keepdims=True)
        dl_acc[...] += gather_heads(jnp.broadcast_to(ends, (8, GW)), sel)[0:1]
        dw_ref[:, glanes] = (dwi[:, glanes] + dot_nt(xt, gst)).astype(BF)
        xt_s[:, lanes] = (dxa[:, lanes] + te * zg).astype(BF)
        pltpu.make_async_copy(xt_s.at[:, lanes], dx_hbm.at[:, lanes], out_sem.at[g]).start()
        return 0

    lax.fori_loop(0, groups, returned, 0)
    rate = -jnp.exp(prm_s[1:2])
    trow = lax.broadcasted_iota(jnp.int32, (BLOCK, heads), 0)
    dwithin = r_acc[...] - c_acc[...] + jnp.where(trow == BLOCK - 1, dl_acc[...], 0.0)
    dld = tri_sum(triangle(True), dwithin)
    draw = (c_acc[...] / step_s[...] + rate * dld) * sig_s[...]
    sums = jnp.concatenate(
        [
            jnp.sum(dld * decay_s[...], axis=0, keepdims=True),
            jnp.sum(draw, axis=0, keepdims=True),
            sk_acc[...],
            jnp.zeros((5, heads), FL),
        ],
        axis=0,
    )
    dstep_ref[...] = draw.astype(BF)
    sums = total(sums, hy, y, ROW, in_row, hy_s, hy_r)
    sums = total(sums, hr, row, rows, in_column, hr_s, hr_r)
    sums = total(sums, hd, d, dps, across, hd_s, hd_r) * factor
    hg_ref[...] = pltpu.roll(sums, lax.rem(heads - c * owned, heads), 1)
    for half in range(2):
        for i in range(1, ROW):
            for k in range(gq):
                out(half, k, (y + i) % ROW, y).wait_send()
                ret(half, k, (y + i) % ROW, y).wait_send()
        for i in range(1, rows):
            up(half, tb, (row + i) % rows, row).wait_send()
            down(half, (row + i) % rows, row).wait_send()

    def written(g, _):
        lanes = pl.ds(pl.multiple_of(g * GW, GW), GW)
        pltpu.make_async_copy(xt_s.at[:, lanes], dx_hbm.at[:, lanes], out_sem.at[g]).wait()
        return 0

    lax.fori_loop(0, groups, written, 0)


def finish(owned, dx_in, dw_in, dr_in, ds_in, hg_in, dx_out, dw_out, dr_out, ds_out, hg_out, dx, dw, dr, ds, sem):
    step = BLOCK // PARTS
    moves = [(dx_in.at[pl.ds(i * step, step)], dx.at[pl.ds(i * step, step)], dx_out.at[pl.ds(i * step, step)]) for i in range(PARTS)]
    moves += [(dw_in, dw, dw_out), (dr_in, dr, dr_out), (ds_in, ds, ds_out)]
    loads = [pltpu.make_async_copy(a, b, sem.at[0, i]) for i, (a, b, _) in enumerate(moves)]
    stores = [pltpu.make_async_copy(b, c, sem.at[1, i]) for i, (_, b, c) in enumerate(moves)]
    for load in loads:
        load.start()
    hg_out[...] = hg_in[:3, :owned]
    for load, store in zip(loads, stores):
        load.wait()
        store.start()
    for store in stores:
        store.wait()


def body(head_inputs, write_proj, read_projection, step_raw, output_grad, decay_log, step_bias, skip_gain):
    n, dps = lax.axis_size("seq"), lax.axis_size("dp")
    x, w, r, raw, dy = head_inputs[0], write_proj[0], read_projection[0], step_raw[0], output_grad[0]
    heads = raw.shape[1]
    groups = heads // PER_GROUP
    owned = heads // n
    factor = 1.0 / math.sqrt(dps * n * BLOCK * HEADDIM)
    vm = pl.BlockSpec(memory_space=pltpu.VMEM)
    sm = pl.BlockSpec(memory_space=pltpu.SMEM)
    hbm = pl.BlockSpec(memory_space=pl.ANY)
    cat2 = pltpu.VMEM((BLOCK, 2 * heads), BF)
    cat1 = pltpu.VMEM((HALF, 2 * heads), BF)
    full = pltpu.VMEM((BLOCK, heads), FL)
    tr = pltpu.VMEM((heads, BLOCK), FL)
    row = pltpu.VMEM((1, heads), FL)
    wide = pltpu.VMEM((BLOCK, GW), FL)
    rows, gq = n // ROW, groups // ROW
    pq = gq * PAIRS
    po = pq // rows

    def small(count):
        return pltpu.VMEM((count, 8, heads), FL)

    sem = pltpu.SemaphoreType.DMA
    dx, dw, dr, dstep, hg = pl.pallas_call(
        functools.partial(kernel, heads, groups, n, dps, factor),
        out_shape=[
            jax.ShapeDtypeStruct(x.shape, BF),
            jax.ShapeDtypeStruct(w.shape, BF),
            jax.ShapeDtypeStruct(r.shape, BF),
            jax.ShapeDtypeStruct(raw.shape, BF),
            jax.ShapeDtypeStruct((8, heads), FL),
        ],
        in_specs=[hbm] * 4 + [vm] + [sm] * 3,
        out_specs=[hbm] + [vm] * 4,
        scratch_shapes=[
            pltpu.VMEM(x.shape, BF), pltpu.VMEM(x.shape, BF), pltpu.VMEM(w.shape, BF), pltpu.VMEM(r.shape, BF),
            pltpu.VMEM((8, heads), FL), pltpu.VMEM((groups, 2 * heads, GW), BF), full, full, full,
            full, tr, tr, cat2, cat2, cat1, cat1,
            pltpu.VMEM((DEC, heads), BF), pltpu.VMEM((8, 2 * heads), BF),
            full, full, row, row,
            pltpu.VMEM(x.shape, FL), wide, wide, pltpu.VMEM(r.shape, FL), pltpu.VMEM(w.shape, FL), pltpu.VMEM(x.shape, BF),
            pltpu.VMEM((2, ROW, pq * 128 + pq * DEC, 128), BF), pltpu.VMEM((2, ROW, pq * 128 + pq * DEC, 128), BF),
            pltpu.VMEM((2, ROW, pq * 128, 128), BF), pltpu.VMEM((2, ROW, pq * 128, 128), BF),
            pltpu.VMEM((ROW, pq, 8, 128), FL),
            pltpu.VMEM((2, rows, po * (128 + DEC), 128), BF), pltpu.VMEM((2, rows, po * (128 + DEC), 128), BF),
            pltpu.VMEM((2, rows, po * 128, 128), BF), pltpu.VMEM((2, rows, po * 128, 128), BF),
            small(ROW), small(rows), small(ROW), small(rows), small(dps),
            sem((4,)), sem((groups,)), sem((2, gq, ROW)), sem((2, gq, ROW)), sem((2, gq, ROW)), sem((2, gq, ROW)),
            sem((2, rows)), sem((2, rows)), sem((2, rows)), sem((2, rows)),
            sem((ROW,)), sem((ROW,)), sem((rows,)), sem((rows,)), sem((ROW,)), sem((ROW,)), sem((rows,)), sem((rows,)),
            sem((dps,)), sem((dps,)),
        ],
        compiler_params=pltpu.CompilerParams(
            collective_id=0, has_side_effects=True, vmem_limit_bytes=60 * 2**20
        ),
        name="mixer_backward",
    )(x, dy, w, r, raw, step_bias, decay_log, skip_gain)
    dx, dw, dr, dstep, hg = pl.pallas_call(
        functools.partial(finish, owned),
        out_shape=[jax.ShapeDtypeStruct(a.shape, BF) for a in (dx, dw, dr, dstep)]
        + [jax.ShapeDtypeStruct((3, owned), FL)],
        in_specs=[hbm] * 4 + [vm],
        out_specs=[hbm] * 4 + [vm],
        scratch_shapes=[pltpu.VMEM(a.shape, BF) for a in (dx, dw, dr, dstep)] + [sem((2, 3 + PARTS))],
        name="results",
    )(dx, dw, dr, dstep, hg)
    return (dx[None], dw[None], dr[None], dstep[None], hg)


def solution(mesh):
    tok = P("dp", "seq", None)
    return jax.shard_map(
        body,
        mesh=mesh,
        in_specs=(tok, tok, tok, tok, tok, P("seq"), P("seq"), P("seq")),
        out_specs=(tok, tok, tok, tok, P(None, "seq")),
        check_vma=False,
    )
```

time: 150 us -> 136 us (0.907)
  local copies, waits for them, and re-layouts: 8.21 us -> 0 us
  Pallas kernels: 141 us -> 135 us
    pallas_call x1, Pallas kernels: 141 us -> 129 us  [body(): pl.pallas_call(functools.partial(kernel, heads, groups, n, dps, factor),...]
    unnamed x10 -> x0, local copies, waits for them, and re-layouts: 6.96 us -> none
    pallas_call x0 -> x1, Pallas kernels: none -> 5.98 us  [body(): pl.pallas_call(functools.partial(finish, owned), out_shape=[jax.ShapeDtyp...]
where the time goes in v4:
time: 136 us
  Pallas kernels  135 us (99%)
    pallas_call x1, Pallas kernels, body(): pl.pallas_call(functools.partial(kernel, heads, groups, n, dps, factor),...  129 us
    pallas_call x1, Pallas kernels, body(): pl.pallas_call(functools.partial(finish, owned), out_shape=[jax.ShapeDtyp...  5.98 us

profile of v4, /device:TPU:1, one launch (start us, length us, event | category | flops | bytes accessed | tf_op | source)
XLA Modules:
  0.0 135.8 jit_solution(6044224127429477356)
XLA Ops:
  0.6 129.0 %mixer_backward.1 = (bf16[256,8192]{1,0:T(8,128)(2,1)}, bf16[256,1024]{1,0:T(8,128)(2,1)}, bf16[256,1024]{1,0:T(8,128)(2,1)}, bf16[256,128]{1,0:T(8,128)(2,1)}, f32[8,128]{1,0:T(8,128)}) custom-call(bf16[256,8192]{1,0:T(8,128)(2,1)} %bitcast.9, bf16[256,8192]{1,0:T(8,128)(2,1)} %bitcast.10, bf16[256,1024]{1,0:T(8,128)(2,1)} %bitcast.11, ...), custom_call_target="tpu_custom_call" | custom-call | tf_op jit(solution)/shard_map/mixer_backward/pallas_call | solution.py:549
  129.6 6.0 %results.1 = (bf16[256,8192]{1,0:T(8,128)(2,1)}, bf16[256,1024]{1,0:T(8,128)(2,1)}, bf16[256,1024]{1,0:T(8,128)(2,1)}, bf16[256,128]{1,0:T(8,128)(2,1)}, f32[3,4]{1,0:T(4,128)}) custom-call(bf16[256,8192]{1,0:T(8,128)(2,1)} %get-tuple-element.15.dx_in, bf16[256,1024]{1,0:T(8,128)(2,1)} %get-tuple-element.16.dw_in, ...), custom_call_target="tpu_custom_call" | custom-call | tf_op jit(solution)/shard_map/results/pallas_call | solution.py:583

commit v5 on v4

--- a/solution.py
+++ b/solution.py
@@ -17,7 +17,7 @@
 GW = PER_GROUP * HEADDIM
 ROW = 4
 DEC = 16
-PARTS = 8
+PARTS = 4
 
 BF = jnp.bfloat16
 FL = jnp.float32
@@ -64,11 +64,9 @@
     return jnp.where(keep, 1.0, 0.0).astype(BF)
 
 
-def spread(g, heads, copies):
-    row = lax.broadcasted_iota(jnp.int32, (copies * heads, GW), 0)
-    col = lax.broadcasted_iota(jnp.int32, (copies * heads, GW), 1)
-    if copies == 2:
-        row = jnp.where(row >= heads, row - heads, row)
+def spread(g, heads):
+    row = lax.broadcasted_iota(jnp.int32, (heads, GW), 0)
+    col = lax.broadcasted_iota(jnp.int32, (heads, GW), 1)
     return jnp.where(row == g * PER_GROUP + col // HEADDIM, 1.0, 0.0).astype(BF)
 
 
@@ -86,16 +84,6 @@
     decay = rate * step
     within = tri_sum(triangle(False), decay)
     return v, step, rate, decay, within
-
-
-def decay_factors(step, within):
-    last = within[BLOCK - 1 : BLOCK]
-    mid = within[HALF - 1 : HALF]
-    to_end = jnp.exp(last - within) * step
-    from_start = jnp.exp(within)
-    to_mid = jnp.exp(mid - within[:HALF]) * step[:HALF]
-    from_mid = jnp.exp(within[HALF:] - mid)
-    return last, to_end, from_start, to_mid, from_mid
 
 
 def last_terms(last):
@@ -178,8 +166,8 @@
     dx_hbm, dw_ref, dr_ref, dstep_ref, hg_ref,
     x_ref, dy_ref, w_ref, r_ref, prm_s, sel_s, step_s, decay_s, sig_s, within_s, wt_s, st_s, te_s, ew_s, tm_s, fm_s, l3_s, full_s,
     r_acc, c_acc, dl_acc, sk_acc, dxa, pr, pc, dri, dwi, xt_s,
-    sd, got, back, cg, es, tb, tgot, cb, crow, py, pr_all, hy, hr, hd,
-    in_sem, out_sem, s1, r1, s2, r2, s3, r3, s4, r4, py_s, py_r, pz_s, pz_r, hy_s, hy_r, hr_s, hr_r, hd_s, hd_r,
+    sd, got, back, cg, es, tb, tgot, cb, crow, py, pr_all, hy, hr,
+    in_sem, out_sem, s1, r1, s2, r2, s3, r3, s4, r4, py_s, py_r, pz_s, pz_r, hy_s, hy_r, hr_s, hr_r,
 ):
     c = lax.axis_index("seq")
     d = lax.axis_index("dp")
@@ -201,21 +189,22 @@
     def in_column(t):
         return {"seq": t * ROW + y}
 
-    def across(t):
-        return {"dp": t}
+    def in_cell(t):
+        return {"seq": row * ROW + t // dps, "dp": t % dps}
 
     barrier = pltpu.get_barrier_semaphore()
     for i in range(1, rows):
         pl.semaphore_signal(barrier, inc=1, device_id=in_column((row + i) % rows), device_id_type=MESH)
-    for i in range(1, dps):
-        pl.semaphore_signal(barrier, inc=1, device_id=across((d + i) % dps), device_id_type=MESH)
-    for i in range(1, ROW):
-        pl.semaphore_signal(barrier, inc=1, device_id=in_row((y + i) % ROW), device_id_type=MESH)
+    cell, at_cell = ROW * dps, y * dps + d
+    for i in range(1, cell):
+        pl.semaphore_signal(barrier, inc=1, device_id=in_cell((at_cell + i) % cell), device_id_type=MESH)
     for g in range(groups):
-        sel_s[g] = spread(g, heads, 2)
+        one = spread(g, heads)
+        sel_s[g, :heads] = one
+        sel_s[g, heads:] = one
     for acc in (r_acc, c_acc, dl_acc, sk_acc):
         acc[...] = jnp.zeros_like(acc)
-    pl.semaphore_wait(barrier, rows - 1 + dps - 1 + ROW - 1)
+    pl.semaphore_wait(barrier, rows - 1 + cell - 1)
 
     lane = lax.broadcasted_iota(jnp.int32, (8, heads), 1)
     which = lax.broadcasted_iota(jnp.int32, (8, heads), 0)
@@ -244,19 +233,24 @@
     mine = total(mine, py, y, ROW, in_row, py_s, py_r)
     prm_s[...] = total(mine, pr_all, row, rows, in_column, pz_s, pz_r)
     v, step, _, decay, within = rates(raw_ref[...], prm_s[...])
+    within_s[...] = within
     step_s[...] = step
     decay_s[...] = decay
     sig_s[...] = 1.0 / (1.0 + jnp.exp(-v))
-    last, to_end, from_start, to_mid, from_mid = decay_factors(step, within)
-    within_s[...] = within
-    wt_s[...] = within.T
-    st_s[...] = step.T
-    te_s[...] = cat_hi_lo(to_end)
-    ew_s[...] = cat_hi_lo(from_start)
-    tm_s[...] = cat_hi_lo(to_mid)
-    fm_s[...] = cat_hi_lo(from_mid)
+    last = within[BLOCK - 1 : BLOCK]
+    te_s[...] = cat_hi_lo(jnp.exp(last - within) * step)
+    ew_s[...] = cat_hi_lo(jnp.exp(within))
     l3_s[...] = last_terms(last)
-    full_s[...] = cat_hi_lo(jnp.concatenate([jnp.exp(last), prm_s[2:3], jnp.zeros((6, heads), FL)], axis=0))
+
+    def rest():
+        within, step = within_s[...], step_s[...]
+        last, mid = within[BLOCK - 1 : BLOCK], within[HALF - 1 : HALF]
+        wt_s[...] = within.T
+        st_s[...] = step.T
+        tm_s[...] = cat_hi_lo(jnp.exp(mid - within[:HALF]) * step[:HALF])
+        fm_s[...] = cat_hi_lo(jnp.exp(within[HALF:] - mid))
+        full_s[...] = cat_hi_lo(jnp.concatenate([jnp.exp(last), prm_s[2:3], jnp.zeros((6, heads), FL)], axis=0))
+
     for load in loads:
         load.wait()
 
@@ -312,6 +306,7 @@
         c_acc[...] += gather_heads(pc[...], sel2[:heads])
         return 0
 
+    rest()
     share = (groups * 5 // 8, groups * 6 // 8, groups * 7 // 8, groups)
     lax.fori_loop(0, share[0], local, 0)
 
@@ -485,9 +480,8 @@
         axis=0,
     )
     dstep_ref[...] = draw.astype(BF)
-    sums = total(sums, hy, y, ROW, in_row, hy_s, hy_r)
-    sums = total(sums, hr, row, rows, in_column, hr_s, hr_r)
-    sums = total(sums, hd, d, dps, across, hd_s, hd_r) * factor
+    sums = total(sums, hy, at_cell, cell, in_cell, hy_s, hy_r)
+    sums = total(sums, hr, row, rows, in_column, hr_s, hr_r) * factor
     hg_ref[...] = pltpu.roll(sums, lax.rem(heads - c * owned, heads), 1)
     for half in range(2):
         for i in range(1, ROW):
@@ -506,17 +500,23 @@
     lax.fori_loop(0, groups, written, 0)
 
 
-def finish(owned, dx_in, dw_in, dr_in, ds_in, hg_in, dx_out, dw_out, dr_out, ds_out, hg_out, dx, dw, dr, ds, sem):
+def finish(
+    owned, dx_in, dw_in, dr_in, ds_in, hg_in, dx_out, dw_out, dr_out, ds_out, hg_out, dx, dw, dr, ds, hg, own, sem
+):
     step = BLOCK // PARTS
-    moves = [(dx_in.at[pl.ds(i * step, step)], dx.at[pl.ds(i * step, step)], dx_out.at[pl.ds(i * step, step)]) for i in range(PARTS)]
+    parts = [pl.ds(i * step, step) for i in range(PARTS)]
+    moves = [(hg_in, hg, hg_out)] + [(dx_in.at[p], dx.at[p], dx_out.at[p]) for p in parts]
     moves += [(dw_in, dw, dw_out), (dr_in, dr, dr_out), (ds_in, ds, ds_out)]
     loads = [pltpu.make_async_copy(a, b, sem.at[0, i]) for i, (a, b, _) in enumerate(moves)]
-    stores = [pltpu.make_async_copy(b, c, sem.at[1, i]) for i, (_, b, c) in enumerate(moves)]
+    stores = [
+        pltpu.make_async_copy(own if i == 0 else b, c, sem.at[1, i]) for i, (_, b, c) in enumerate(moves)
+    ]
     for load in loads:
         load.start()
-    hg_out[...] = hg_in[:3, :owned]
-    for load, store in zip(loads, stores):
+    for i, (load, store) in enumerate(zip(loads, stores)):
         load.wait()
+        if i == 0:
+            own[...] = hg[:3, :owned]
         store.start()
     for store in stores:
         store.wait()
@@ -569,11 +569,11 @@
             pltpu.VMEM((ROW, pq, 8, 128), FL),
             pltpu.VMEM((2, rows, po * (128 + DEC), 128), BF), pltpu.VMEM((2, rows, po * (128 + DEC), 128), BF),
             pltpu.VMEM((2, rows, po * 128, 128), BF), pltpu.VMEM((2, rows, po * 128, 128), BF),
-            small(ROW), small(rows), small(ROW), small(rows), small(dps),
+            small(ROW), small(rows), small(ROW * dps), small(rows),
             sem((4,)), sem((groups,)), sem((2, gq, ROW)), sem((2, gq, ROW)), sem((2, gq, ROW)), sem((2, gq, ROW)),
             sem((2, rows)), sem((2, rows)), sem((2, rows)), sem((2, rows)),
-            sem((ROW,)), sem((ROW,)), sem((rows,)), sem((rows,)), sem((ROW,)), sem((ROW,)), sem((rows,)), sem((rows,)),
-            sem((dps,)), sem((dps,)),
+            sem((ROW,)), sem((ROW,)), sem((rows,)), sem((rows,)),
+            sem((ROW * dps,)), sem((ROW * dps,)), sem((rows,)), sem((rows,)),
         ],
         compiler_params=pltpu.CompilerParams(
             collective_id=0, has_side_effects=True, vmem_limit_bytes=60 * 2**20
@@ -584,9 +584,10 @@
         functools.partial(finish, owned),
         out_shape=[jax.ShapeDtypeStruct(a.shape, BF) for a in (dx, dw, dr, dstep)]
         + [jax.ShapeDtypeStruct((3, owned), FL)],
-        in_specs=[hbm] * 4 + [vm],
-        out_specs=[hbm] * 4 + [vm],
-        scratch_shapes=[pltpu.VMEM(a.shape, BF) for a in (dx, dw, dr, dstep)] + [sem((2, 3 + PARTS))],
+        in_specs=[hbm] * 5,
+        out_specs=[hbm] * 5,
+        scratch_shapes=[pltpu.VMEM(a.shape, BF) for a in (dx, dw, dr, dstep)]
+        + [pltpu.VMEM(hg.shape, FL), pltpu.VMEM((3, owned), FL), sem((2, 4 + PARTS))],
         name="results",
     )(dx, dw, dr, dstep, hg)
     return (dx[None], dw[None], dr[None], dstep[None], hg)

time: 136 us -> 132 us (0.971)
  Pallas kernels: 135 us -> 131 us
    pallas_call x1, Pallas kernels: 129 us -> 126 us  [body(): pl.pallas_call(functools.partial(kernel, heads, groups, n, dps, factor),...]
    pallas_call x1, Pallas kernels: 5.98 us -> 4.23 us  [body(): pl.pallas_call(functools.partial(finish, owned), out_shape=[jax.ShapeDtyp...]
where the time goes in v5:
time: 132 us; the launch traced here: 131 us
  Pallas kernels  131 us (99%)
    pallas_call x1, Pallas kernels, body(): pl.pallas_call(functools.partial(kernel, heads, groups, n, dps, factor),...  126 us
    pallas_call x1, Pallas kernels, body(): pl.pallas_call(functools.partial(finish, owned), out_shape=[jax.ShapeDtyp...  4.23 us

profile of v5, /device:TPU:1, one launch (start us, length us, event | category | flops | bytes accessed | tf_op | source)
XLA Modules:
  0.0 131.4 jit_solution(3183023960545084876)
XLA Ops:
  0.6 126.4 %mixer_backward.1 = (bf16[256,8192]{1,0:T(8,128)(2,1)}, bf16[256,1024]{1,0:T(8,128)(2,1)}, bf16[256,1024]{1,0:T(8,128)(2,1)}, bf16[256,128]{1,0:T(8,128)(2,1)}, f32[8,128]{1,0:T(8,128)}) custom-call(bf16[256,8192]{1,0:T(8,128)(2,1)} %bitcast.9, bf16[256,8192]{1,0:T(8,128)(2,1)} %bitcast.10, bf16[256,1024]{1,0:T(8,128)(2,1)} %bitcast.11, ...), custom_call_target="tpu_custom_call" | custom-call | tf_op jit(solution)/shard_map/mixer_backward/pallas_call | solution.py:549
  127.0 4.2 %results.1 = (bf16[256,8192]{1,0:T(8,128)(2,1)}, bf16[256,1024]{1,0:T(8,128)(2,1)}, bf16[256,1024]{1,0:T(8,128)(2,1)}, bf16[256,128]{1,0:T(8,128)(2,1)}, f32[3,4]{1,0:T(4,128)}) custom-call(bf16[256,8192]{1,0:T(8,128)(2,1)} %get-tuple-element.15.dx_in, bf16[256,1024]{1,0:T(8,128)(2,1)} %get-tuple-element.16.dw_in, ...), custom_call_target="tpu_custom_call" | custom-call | tf_op jit(solution)/shard_map/results/pallas_call | solution.py:583

commit v6 on v5

--- a/solution.py
+++ b/solution.py
@@ -163,11 +163,11 @@
 def kernel(
     heads, groups, n, dps, factor,
     x_hbm, dy_hbm, w_hbm, r_hbm, raw_ref, bias_ref, dlog_ref, gain_ref,
-    dx_hbm, dw_ref, dr_ref, dstep_ref, hg_ref,
-    x_ref, dy_ref, w_ref, r_ref, prm_s, sel_s, step_s, decay_s, sig_s, within_s, wt_s, st_s, te_s, ew_s, tm_s, fm_s, l3_s, full_s,
+    dx_hbm, dw_hbm, dr_hbm, ds_hbm, hg_ref,
+    dw_ref, dr_ref, dstep_ref, x_ref, dy_ref, w_ref, r_ref, prm_s, sel_s, step_s, decay_s, sig_s, within_s, wt_s, st_s, te_s, ew_s, tm_s, fm_s, l3_s, full_s,
     r_acc, c_acc, dl_acc, sk_acc, dxa, pr, pc, dri, dwi, xt_s,
     sd, got, back, cg, es, tb, tgot, cb, crow, py, pr_all, hy, hr,
-    in_sem, out_sem, s1, r1, s2, r2, s3, r3, s4, r4, py_s, py_r, pz_s, pz_r, hy_s, hy_r, hr_s, hr_r,
+    in_sem, out_sem, end_sem, s1, r1, s2, r2, s3, r3, s4, r4, py_s, py_r, pz_s, pz_r, hy_s, hy_r, hr_s, hr_r,
 ):
     c = lax.axis_index("seq")
     d = lax.axis_index("dp")
@@ -443,6 +443,11 @@
         return 0
 
     lax.fori_loop(0, groups, carried, 0)
+    ends = [
+        pltpu.make_async_copy(a, b, end_sem.at[i])
+        for i, (a, b) in enumerate(((dr_ref, dr_hbm), (dw_ref, dw_hbm), (dstep_ref, ds_hbm)))
+    ]
+    ends[0].start()
 
     def returned(j, _):
         k, t = j // ROW, (y + j) % ROW
@@ -465,6 +470,7 @@
         return 0
 
     lax.fori_loop(0, groups, returned, 0)
+    ends[1].start()
     rate = -jnp.exp(prm_s[1:2])
     trow = lax.broadcasted_iota(jnp.int32, (BLOCK, heads), 0)
     dwithin = r_acc[...] - c_acc[...] + jnp.where(trow == BLOCK - 1, dl_acc[...], 0.0)
@@ -480,6 +486,7 @@
         axis=0,
     )
     dstep_ref[...] = draw.astype(BF)
+    ends[2].start()
     sums = total(sums, hy, at_cell, cell, in_cell, hy_s, hy_r)
     sums = total(sums, hr, row, rows, in_column, hr_s, hr_r) * factor
     hg_ref[...] = pltpu.roll(sums, lax.rem(heads - c * owned, heads), 1)
@@ -498,6 +505,8 @@
         return 0
 
     lax.fori_loop(0, groups, written, 0)
+    for end in ends:
+        end.wait()
 
 
 def finish(
@@ -556,8 +565,9 @@
             jax.ShapeDtypeStruct((8, heads), FL),
         ],
         in_specs=[hbm] * 4 + [vm] + [sm] * 3,
-        out_specs=[hbm] + [vm] * 4,
+        out_specs=[hbm] * 4 + [vm],
         scratch_shapes=[
+            pltpu.VMEM(w.shape, BF), pltpu.VMEM(r.shape, BF), pltpu.VMEM(raw.shape, BF),
             pltpu.VMEM(x.shape, BF), pltpu.VMEM(x.shape, BF), pltpu.VMEM(w.shape, BF), pltpu.VMEM(r.shape, BF),
             pltpu.VMEM((8, heads), FL), pltpu.VMEM((groups, 2 * heads, GW), BF), full, full, full,
             full, tr, tr, cat2, cat2, cat1, cat1,
@@ -570,7 +580,7 @@
             pltpu.VMEM((2, rows, po * (128 + DEC), 128), BF), pltpu.VMEM((2, rows, po * (128 + DEC), 128), BF),
             pltpu.VMEM((2, rows, po * 128, 128), BF), pltpu.VMEM((2, rows, po * 128, 128), BF),
             small(ROW), small(rows), small(ROW * dps), small(rows),
-            sem((4,)), sem((groups,)), sem((2, gq, ROW)), sem((2, gq, ROW)), sem((2, gq, ROW)), sem((2, gq, ROW)),
+            sem((4,)), sem((groups,)), sem((3,)), sem((2, gq, ROW)), sem((2, gq, ROW)), sem((2, gq, ROW)), sem((2, gq, ROW)),
             sem((2, rows)), sem((2, rows)), sem((2, rows)), sem((2, rows)),
             sem((ROW,)), sem((ROW,)), sem((rows,)), sem((rows,)),
             sem((ROW * dps,)), sem((ROW * dps,)), sem((rows,)), sem((rows,)),

time: 132 us -> 131 us (level)
  no operation moved by 1% of the time
where the time goes in v6:
time: 131 us
  Pallas kernels  130 us (99%)
    pallas_call x1, Pallas kernels, body(): pl.pallas_call(functools.partial(kernel, heads, groups, n, dps, factor),...  126 us
    pallas_call x1, Pallas kernels, body(): pl.pallas_call(functools.partial(finish, owned), out_shape=[jax.ShapeDtyp...  4.23 us

profile of v6, /device:TPU:1, one launch (start us, length us, event | category | flops | bytes accessed | tf_op | source)
XLA Modules:
  0.0 131.0 jit_solution(4760808234749510913)
XLA Ops:
  0.6 126.0 %mixer_backward.1 = (bf16[256,8192]{1,0:T(8,128)(2,1)}, bf16[256,1024]{1,0:T(8,128)(2,1)}, bf16[256,1024]{1,0:T(8,128)(2,1)}, bf16[256,128]{1,0:T(8,128)(2,1)}, f32[8,128]{1,0:T(8,128)}) custom-call(bf16[256,8192]{1,0:T(8,128)(2,1)} %bitcast.9, bf16[256,8192]{1,0:T(8,128)(2,1)} %bitcast.10, bf16[256,1024]{1,0:T(8,128)(2,1)} %bitcast.11, ...), custom_call_target="tpu_custom_call" | custom-call | tf_op jit(solution)/shard_map/mixer_backward/pallas_call | solution.py:558
  126.6 4.2 %results.1 = (bf16[256,8192]{1,0:T(8,128)(2,1)}, bf16[256,1024]{1,0:T(8,128)(2,1)}, bf16[256,1024]{1,0:T(8,128)(2,1)}, bf16[256,128]{1,0:T(8,128)(2,1)}, f32[3,4]{1,0:T(4,128)}) custom-call(bf16[256,8192]{1,0:T(8,128)(2,1)} %get-tuple-element.15.dx_in, bf16[256,1024]{1,0:T(8,128)(2,1)} %get-tuple-element.16.dw_in, ...), custom_call_target="tpu_custom_call" | custom-call | tf_op jit(solution)/shard_map/results/pallas_call | solution.py:593

commit v7 on v6

--- a/solution.py
+++ b/solution.py
@@ -226,20 +226,19 @@
         for i in range(1, count):
             copy(i, me).start()
         for i in range(1, count):
+            copy(i, (me + i) % count).wait_recv()
+        out = jnp.sum(buf[...], axis=0)
+        for i in range(1, count):
             copy(i, me).wait_send()
-            copy(i, (me + i) % count).wait_recv()
-        return jnp.sum(buf[...], axis=0)
+        return out
 
     mine = total(mine, py, y, ROW, in_row, py_s, py_r)
     prm_s[...] = total(mine, pr_all, row, rows, in_column, pz_s, pz_r)
     v, step, _, decay, within = rates(raw_ref[...], prm_s[...])
     within_s[...] = within
     step_s[...] = step
-    decay_s[...] = decay
-    sig_s[...] = 1.0 / (1.0 + jnp.exp(-v))
     last = within[BLOCK - 1 : BLOCK]
     te_s[...] = cat_hi_lo(jnp.exp(last - within) * step)
-    ew_s[...] = cat_hi_lo(jnp.exp(within))
     l3_s[...] = last_terms(last)
 
     def rest():
@@ -276,6 +275,10 @@
                 sd[0, t, at : at + DEC, :] = lx[:, p * 128 : p * 128 + 128]
 
     for half in range(2):
+        if half == 1:
+            ew_s[...] = cat_hi_lo(jnp.exp(within_s[...]))
+            decay_s[...] = decay
+            sig_s[...] = 1.0 / (1.0 + jnp.exp(-v))
         for k in range(gq):
 
             def send(i, _):
@@ -403,8 +406,15 @@
                 return 0
 
             lax.fori_loop(0, PAIRS, one, 0)
-            for i in range(1, ROW):
-                ret(half, k, (y + i) % ROW, y).start()
+            if half == 0:
+                for i in range(1, ROW):
+                    ret(half, k, (y + i) % ROW, y).start()
+            else:
+                ret(half, k, (y + 2) % ROW, y).start()
+        if half == 1:
+            for k in range(gq):
+                for i in (1, 3):
+                    ret(half, k, (y + i) % ROW, y).start()
         cg[half, y] = back[half, y]
 
     row_totals(0)
@@ -450,7 +460,9 @@
     ends[0].start()
 
     def returned(j, _):
-        k, t = j // ROW, (y + j) % ROW
+        late = j // 4
+        k = (1 - late) * (j % 2) + late * (j % 4 // 2)
+        t = (y + (1 - late) * (j // 2 * 2) + late * (1 + j % 2 * 2)) % ROW
         g = t * gq + k
         landed(1, k, t)
         lanes, glanes = slices(g)

time: 131 us -> 130 us (level)
    pallas_call x1, Pallas kernels: 126 us -> 125 us  [body(): pl.pallas_call(functools.partial(kernel, heads, groups, n, dps, factor),...]
where the time goes in v7:
time: 130 us
  Pallas kernels  129 us (99%)
    pallas_call x1, Pallas kernels, body(): pl.pallas_call(functools.partial(kernel, heads, groups, n, dps, factor),...  125 us
    pallas_call x1, Pallas kernels, body(): pl.pallas_call(functools.partial(finish, owned), out_shape=[jax.ShapeDtyp...  4.23 us

profile of v7, /device:TPU:1, one launch (start us, length us, event | category | flops | bytes accessed | tf_op | source)
XLA Modules:
  0.0 129.6 jit_solution(3124770689165198163)
XLA Ops:
  0.6 124.5 %mixer_backward.1 = (bf16[256,8192]{1,0:T(8,128)(2,1)}, bf16[256,1024]{1,0:T(8,128)(2,1)}, bf16[256,1024]{1,0:T(8,128)(2,1)}, bf16[256,128]{1,0:T(8,128)(2,1)}, f32[8,128]{1,0:T(8,128)}) custom-call(bf16[256,8192]{1,0:T(8,128)(2,1)} %bitcast.9, bf16[256,8192]{1,0:T(8,128)(2,1)} %bitcast.10, bf16[256,1024]{1,0:T(8,128)(2,1)} %bitcast.11, ...), custom_call_target="tpu_custom_call" | custom-call | tf_op jit(solution)/shard_map/mixer_backward/pallas_call | solution.py:570
  125.2 4.2 %results.1 = (bf16[256,8192]{1,0:T(8,128)(2,1)}, bf16[256,1024]{1,0:T(8,128)(2,1)}, bf16[256,1024]{1,0:T(8,128)(2,1)}, bf16[256,128]{1,0:T(8,128)(2,1)}, f32[3,4]{1,0:T(4,128)}) custom-call(bf16[256,8192]{1,0:T(8,128)(2,1)} %get-tuple-element.15.dx_in, bf16[256,1024]{1,0:T(8,128)(2,1)} %get-tuple-element.16.dw_in, ...), custom_call_target="tpu_custom_call" | custom-call | tf_op jit(solution)/shard_map/results/pallas_call | solution.py:605
